TPU v7x, 32 devices: a whole 2x2x4 slice. The times are simulated.
32 devices in a mesh: dp: 8 (over z, y), row: 2 (over x), col: 2 (over core).
Axes of the slice: x: 2, y: 2, z: 4, core: 2. Of those that a mesh axis runs over, the one named last changes fastest.
Arguments:
- inputs: bfloat16 [150, 192, 2000], P(None, 'dp', 'row'), may hold values from -6 to 6
- w_second: bfloat16 [2000, 2000], P('row', 'col'), may hold values from -0.125 to 0.125
- gain_second: float32 [2000], P('col'), may hold values from 0.5 to 1.5
- shift_second: float32 [2000], P('col'), may hold values from -3 to 3
- recur_second: float32 [2000], P('col'), may hold values from 0.2 to 0.9
- w_third: bfloat16 [2000, 2000], P('col', 'row'), may hold values from -0.125 to 0.125
- gain_third: float32 [2000], P('row'), may hold values from 0.5 to 1.5
- shift_third: float32 [2000], P('row'), may hold values from -3 to 3
- recur_third: float32 [2000], P('row'), may hold values from 0.2 to 0.9
- cotangent: bfloat16 [150, 192, 2000], P(None, ('dp', 'col'), 'row'), may hold values from -6 to 6
Outputs:
- output: float32 [150, 192, 2000], P(None, ('dp', 'col'), 'row')
- grad_inputs: float32 [150, 192, 2000], P(None, ('dp', 'col'), 'row')
- grad_w_second: float32 [2000, 2000], P('row', 'col')
- grad_gain_second: float32 [2000], P('col')
- grad_shift_second: float32 [2000], P('col')
- grad_recur_second: float32 [2000], P('col')
- grad_w_third: float32 [2000, 2000], P('col', 'row')
- grad_gain_third: float32 [2000], P('row')
- grad_shift_third: float32 [2000], P('row')
- grad_recur_third: float32 [2000], P('row')
All inputs are finite; a program needn't handle non-finite values.
Results may differ from a plain program's by a relative error of at most 0.0065.
Values may be sent and summed in bfloat16 or wider, within the bound.
No kernel may reach another device: no remote copies, remote signals or barrier semaphores. Data moves between devices by JAX's collectives and lax.ppermute only.
A program may use at most 256 MiB of HBM per device.

v0:
```python
import jax
import jax.numpy as jnp
from jax import lax
from jax.sharding import PartitionSpec as P

norm_eps = 1e-05


def run_recurrence(pre_norm, recur):

    def advance(state, column):
        fresh = jax.nn.gelu(column + recur * state)
        return (fresh, fresh)

    start = jnp.zeros(pre_norm.shape[1:], jnp.float32)
    _, states = lax.scan(advance, start, pre_norm, unroll=5)
    return states


def back_recurrence(pre_norm, states, recur, upstream):
    start = jnp.zeros(pre_norm.shape[1:], jnp.float32)
    earlier = jnp.concatenate([start[None], states[:-1]], axis=0)
    argument = pre_norm + recur * earlier
    _, slope_pull = jax.vjp(jax.nn.gelu, argument)
    (slopes,) = slope_pull(jnp.ones_like(argument))

    def retreat(carry, items):
        grad_now, slope_now = items
        arg_grad = (grad_now + carry) * slope_now
        return (recur * arg_grad, arg_grad)

    _, arg_grads = lax.scan(retreat, start, (upstream, slopes), reverse=True, unroll=5)
    return (arg_grads, jnp.sum(arg_grads * earlier, axis=(0, 1)))


def normalize(proj, sums, squares, count, gain, shift):
    mean = sums / count
    var = squares / count - mean * mean
    scale = lax.rsqrt(var + norm_eps)
    unit = (proj - mean) * scale
    return (gain * unit + shift, unit, scale)


def norm_back(norm_grad, unit, scale, gain, gain_grad, shift_grad, count):
    return gain * scale * (norm_grad - shift_grad / count - unit * gain_grad / count)


def moments(proj):
    return (jnp.sum(proj, axis=(0, 1)), jnp.sum(proj * proj, axis=(0, 1)))


def on_device(
    inputs,
    w_second,
    gain_second,
    shift_second,
    recur_second,
    w_third,
    gain_third,
    shift_third,
    recur_third,
    cotangent,
):
    steps, seq_dev, in_width = inputs.shape
    count_all = steps * seq_dev * lax.axis_size("dp")
    partial_second = jnp.einsum("tsi,ij->tsj", inputs, w_second, preferred_element_type=jnp.float32)
    proj_second = lax.psum_scatter(partial_second, "row", scatter_dimension=1, tiled=True)
    sum_second, square_second = lax.psum(moments(proj_second), ("dp", "row"))
    norm_second, unit_second, scale_second = normalize(
        proj_second, sum_second, square_second, count_all, gain_second, shift_second
    )
    states_second = run_recurrence(norm_second, recur_second)
    hidden_low = states_second.astype(jnp.bfloat16)
    hidden_full = lax.all_gather(hidden_low, "row", axis=1, tiled=True)
    partial_third = jnp.einsum(
        "tsi,ij->tsj", hidden_full, w_third, preferred_element_type=jnp.float32
    )
    proj_third = lax.psum_scatter(partial_third, "col", scatter_dimension=1, tiled=True)
    sum_third, square_third = lax.psum(moments(proj_third), ("dp", "col"))
    norm_third, unit_third, scale_third = normalize(
        proj_third, sum_third, square_third, count_all, gain_third, shift_third
    )
    states_third = run_recurrence(norm_third, recur_third)
    share = proj_third.shape[1]
    own_inputs = lax.dynamic_slice_in_dim(inputs, lax.axis_index("col") * share, share, 1).astype(
        jnp.float32
    )
    output = own_inputs + states_third
    upstream = cotangent.astype(jnp.float32)
    norm_grad_third, recur_part_third = back_recurrence(
        norm_third, states_third, recur_third, upstream
    )
    gain_grad_third, shift_grad_third, recur_grad_third = lax.psum(
        (
            jnp.sum(norm_grad_third * unit_third, axis=(0, 1)),
            jnp.sum(norm_grad_third, axis=(0, 1)),
            recur_part_third,
        ),
        ("dp", "col"),
    )
    proj_grad_third = norm_back(
        norm_grad_third,
        unit_third,
        scale_third,
        gain_third,
        gain_grad_third,
        shift_grad_third,
        count_all,
    ).astype(jnp.bfloat16)
    proj_grad_full = lax.all_gather(proj_grad_third, "col", axis=1, tiled=True)
    weight_grad_third = jnp.einsum(
        "tsi,tsj->ij", hidden_full, proj_grad_full, preferred_element_type=jnp.float32
    )
    partial_hidden = jnp.einsum(
        "tsj,ij->tsi", proj_grad_full, w_third, preferred_element_type=jnp.float32
    )
    hidden_grad = lax.psum_scatter(partial_hidden, "row", scatter_dimension=1, tiled=True)
    norm_grad_second, recur_part_second = back_recurrence(
        norm_second, states_second, recur_second, hidden_grad
    )
    gain_grad_second, shift_grad_second, recur_grad_second = lax.psum(
        (
            jnp.sum(norm_grad_second * unit_second, axis=(0, 1)),
            jnp.sum(norm_grad_second, axis=(0, 1)),
            recur_part_second,
        ),
        ("dp", "row"),
    )
    proj_grad_second = norm_back(
        norm_grad_second,
        unit_second,
        scale_second,
        gain_second,
        gain_grad_second,
        shift_grad_second,
        count_all,
    ).astype(jnp.bfloat16)
    second_grad_full = lax.all_gather(proj_grad_second, "row", axis=1, tiled=True)
    weight_grad_second = jnp.einsum(
        "tsi,tsj->ij", inputs, second_grad_full, preferred_element_type=jnp.float32
    )
    partial_inputs = jnp.einsum(
        "tsj,ij->tsi", second_grad_full, w_second, preferred_element_type=jnp.float32
    )
    input_grad = lax.psum_scatter(partial_inputs, "col", scatter_dimension=1, tiled=True) + upstream
    weight_grad_second, weight_grad_third = lax.psum((weight_grad_second, weight_grad_third), "dp")
    return (
        output,
        input_grad,
        weight_grad_second,
        gain_grad_second,
        shift_grad_second,
        recur_grad_second,
        weight_grad_third,
        gain_grad_third,
        shift_grad_third,
        recur_grad_third,
    )


def solution(mesh):
    in_specs = (
        P(None, "dp", "row"),
        P("row", "col"),
        P("col"),
        P("col"),
        P("col"),
        P("col", "row"),
        P("row"),
        P("row"),
        P("row"),
        P(None, ("dp", "col"), "row"),
    )
    out_specs = (
        P(None, ("dp", "col"), "row"),
        P(None, ("dp", "col"), "row"),
        P("row", "col"),
        P("col"),
        P("col"),
        P("col"),
        P("col", "row"),
        P("row"),
        P("row"),
        P("row"),
    )
    return jax.shard_map(
        on_device, mesh=mesh, in_specs=in_specs, out_specs=out_specs, check_vma=False
    )
```

profile of v0, /device:TPU:0, one launch (start us, length us, event | category | flops | bytes accessed | tf_op | source)
XLA Modules:
  0.0 1773.0 jit_solution(6514110791605012885)
XLA Ops:
  7.2 25.3 %fusion.124 = f32[150,24,1000]{2,0,1:T(8,128)} fusion(bf16[150,24,1000]{2,1,0:T(8,128)(2,1)} %param.18, bf16[1000,1000]{1,0:T(8,128)(2,1)} %param.19), kind=kOutput, calls=%fused_computation.209 | convolution fusion | flops 7200000000 | bytes 23600000 | tf_op jit(solution)/shard_map/tsi,ij->tsj/dot_general | solution.py:66
  32.6 172.7 %reduce-scatter.5.cloned.1.call-done = f32[150,12,1000]{2,0,1:T(8,128)} async-done(((f32[150,24,1000]{2,0,1:T(8,128)}), f32[150,12,1000]{2,0,1:T(8,128)}) %reduce-scatter.5.cloned.1.call-update) | async-done | bytes 7200016 | tf_op jit(solution)/shard_map/reduce_scatter | solution.py:67
  209.3 41.5 %all-reduce.5 = (f32[1000]{0:T(1024)S(1)}, f32[1000]{0:T(1024)S(1)}) all-reduce(f32[1000]{0:T(1024)S(1)} %get-tuple-element.449, f32[1000]{0:T(1024)S(1)} %get-tuple-element.448), channel_id=1, replica_groups=mesh['dp'=8,'row'=2,'col'=2] {'dp','row'}, use_global_device_ids=true, to_apply=%region_4.0 | all-reduce | flops 2000 | bytes 16000 | tf_op jit(solution)/shard_map/psum | solution.py:68
  251.4 11.1 multiply_add_fusion.1
  262.6 4.9 broadcast.90.clone.1
  267.5 159.5 %while.60 = (s32[]{:T(128)}, f32[12,1000]{1,0:T(8,128)S(1)}, f32[30,5,12,1000]{3,2,1,0:T(8,128)}, f32[30,5,12,1000]{3,2,1,0:T(8,128)}, f32[1000]{0:T(1024)S(1)},...) while((s32[]{:T(128)}, f32[12,1000]{1,0:T(8,128)S(1)}, ...), condition=%wide.region_6.7_spmd.clone, body=%wide.region_5.6_spmd.clone.sunk | while | flops 852006 | bytes 1759219 | solution.py:16
  427.0 4.6 bitcast_convert_fusion
  436.0 89.2 %all-gather.4.cloned.1.call-done = bf16[150,24,1000]{2,0,1:T(8,128)(2,1)} async-done(((bf16[150,12,1000]{2,0,1:T(8,128)(2,1)}), bf16[150,24,1000]{2,0,1:T(8,128)(2,1)}) %all-gather.4.cloned.1.call-update) | async-done | bytes 7200016 | tf_op jit(solution)/shard_map/all_gather | solution.py:74
  525.2 14.3 fusion.133
  539.7 9.4 copy.54
  549.1 15.0 reduce-scatter.7.cloned.1.call-done
  568.0 34.4 %all-reduce.3 = (f32[1000]{0:T(1024)S(1)}, f32[1000]{0:T(1024)S(1)}) all-reduce(f32[1000]{0:T(1024)S(1)} %get-tuple-element.447, f32[1000]{0:T(1024)S(1)} %get-tuple-element.446), channel_id=1, replica_groups=mesh['dp'=8,'row'=2,'col'=2] {'dp','col'}, use_global_device_ids=true, to_apply=%region_11.12 | all-reduce | flops 2000 | bytes 16000 | tf_op jit(solution)/shard_map/psum | solution.py:79
  602.5 11.2 multiply_add_fusion
  613.7 4.9 broadcast.90.clone
  618.6 159.6 %while.61 = (s32[]{:T(128)}, f32[12,1000]{1,0:T(8,128)S(1)}, f32[30,5,12,1000]{3,2,1,0:T(8,128)}, f32[30,5,12,1000]{3,2,1,0:T(8,128)}, f32[1000]{0:T(1024)S(1)},...) while((s32[]{:T(128)}, f32[12,1000]{1,0:T(8,128)S(1)}, ...), condition=%wide.region_13.14_spmd.clone, body=%wide.region_12.13_spmd.clone.sunk | while | flops 852006 | bytes 1759219 | solution.py:16
  778.2 9.6 slice.278
  787.8 13.6 fusion.105
  801.4 5.0 broadcast.90.clone.2
  806.4 60.3 %while.62 = (s32[]{:T(128)}, f32[12,1000]{1,0:T(8,128)S(1)}, f32[30,5,12,1000]{3,2,1,0:T(8,128)}, f32[1000]{0:T(1024)S(1)}, f32[30,5,12,1000]{3,2,1,0:T(8,128)},...) while((s32[]{:T(128)}, f32[12,1000]{1,0:T(8,128)S(1)}, ...), condition=%wide.region_15.16_spmd.clone, body=%wide.region_14.15_spmd.clone.sunk | while | flops 192007 | bytes 2117403 | solution.py:32
  866.6 4.5 reduce_sum.94
  871.1 15.1 fusion.121
  886.2 57.9 %all-reduce.2 = (f32[1000]{0:T(1024)S(1)}, f32[1000]{0:T(1024)S(1)}, f32[1000]{0:T(1024)}) all-reduce(f32[1000]{0:T(1024)S(1)} %get-tuple-element.443, f32[1000]{0:T(1024)S(1)} %reduce_sum.94, f32[1000]{0:T(1024)S(1)} %get-tuple-element.442), channel_id=1, replica_groups=mesh['dp'=8,'row'=2,'col'=2] {'dp','col'}, use_global_device_ids=true, to_apply=%region_19.20 | all-reduce | flops 3000 | bytes 24000 | tf_op jit(solution)/shard_map/psum | solution.py:93
  944.0 14.0 fusion.119
  958.1 6.3 copy.55
  964.5 15.8 all-gather.6.cloned.1.call-done
  980.3 14.4 fusion.131
  994.8 4.8 slice.279
  999.6 4.5 copy-done.2
  1004.1 12.5 fusion.111
  1016.5 149.4 %reduce-scatter.9.cloned.1.call-done = f32[150,12,1000]{2,0,1:T(8,128)} async-done(((f32[150,24,1000]{2,0,1:T(8,128)}), f32[150,12,1000]{2,0,1:T(8,128)}) %reduce-scatter.9.cloned.1.call-update) | async-done | bytes 7200016 | tf_op jit(solution)/shard_map/reduce_scatter | solution.py:117
  1165.9 11.2 copy.58
  1177.1 5.0 broadcast.90
  1182.1 60.3 %while.63 = (s32[]{:T(128)}, f32[12,1000]{1,0:T(8,128)S(1)}, f32[30,5,12,1000]{3,2,1,0:T(8,128)}, f32[1000]{0:T(1024)S(1)}, f32[30,5,12,1000]{3,2,1,0:T(8,128)},...) while((s32[]{:T(128)}, f32[12,1000]{1,0:T(8,128)S(1)}, ...), condition=%wide.region_22.23_spmd.clone, body=%wide.region_21.22_spmd.clone.sunk | while | flops 192007 | bytes 2117403 | solution.py:32
  1242.4 4.5 reduce_sum.96
  1246.9 15.3 fusion.116
  1262.2 75.9 %all-reduce.4 = (f32[1000]{0:T(1024)S(1)}, f32[1000]{0:T(1024)S(1)}, f32[1000]{0:T(1024)}) all-reduce(f32[1000]{0:T(1024)S(1)} %get-tuple-element.445, f32[1000]{0:T(1024)S(1)} %reduce_sum.96, f32[1000]{0:T(1024)S(1)} %get-tuple-element.444), channel_id=1, replica_groups=mesh['dp'=8,'row'=2,'col'=2] {'dp','row'}, use_global_device_ids=true, to_apply=%region_26.27 | all-reduce | flops 3000 | bytes 24000 | tf_op jit(solution)/shard_map/psum | solution.py:121
  1338.1 14.0 fusion.114
  1352.1 6.3 copy.59
  1358.4 15.6 convolution_bitcast_fusion
  1374.0 74.0 %all-gather.8.cloned.1.call-done = bf16[150,24,1000]{2,0,1:T(8,128)(2,1)} async-done(((bf16[150,12,1000]{2,0,1:T(8,128)(2,1)}), bf16[150,24,1000]{2,0,1:T(8,128)(2,1)}) %all-gather.8.cloned.1.call-update) | async-done | bytes 7200016 | tf_op jit(solution)/shard_map/all_gather | solution.py:138
  1448.1 14.5 fusion.128
  1462.7 14.6 fusion.135
  1477.4 12.6 convert_add_fusion
  1489.9 11.3 copy.63
  1501.2 227.4 %all-reduce.9.cloned.1.call-done = (f32[1000,1000]{0,1:T(8,128)}, f32[1000,1000]{1,0:T(8,128)}) async-done(((f32[1000,1000]{0,1:T(8,128)}, f32[1000,1000]{1,0:T(8,128)}), (f32[1000,1000]{0,1:T(8,128)}, f32[1000,1000]{1,0:T(8,128)})) %all-reduce.9.cloned.1.call-update) | async-done | bytes 8000016 | tf_op jit(solution)/shard_map/psum | solution.py:146
  1728.6 5.4 copy.64
  1734.0 20.4 %reduce-scatter.11.cloned.1.call-done = f32[150,12,1000]{2,0,1:T(8,128)} async-done(((f32[150,24,1000]{2,0,1:T(8,128)}), f32[150,12,1000]{2,0,1:T(8,128)}) %reduce-scatter.11.cloned.1.call-update) | async-done | bytes 7200016 | tf_op jit(solution)/shard_map/reduce_scatter | solution.py:145
  1754.3 9.4 convert_add_fusion.1
  (844 shorter events, 452.3 us)
Async XLA Ops:
  7.2 518.0 %copy-start = (bf16[1000,1000]{1,0:T(8,128)(2,1)S(1)}, bf16[1000,1000]{1,0:T(8,128)(2,1)}, u32[]{:S(2)}) copy-start(bf16[1000,1000]{1,0:T(8,128)(2,1)} %param.23) | copy-start | bytes 6000004
  7.2 198.1 %reduce-scatter.5.cloned.1.call-start = ((), (), s32[]{:S(2)}) async-start(), calls=%async_computation.4 | async-start | bytes 22413312 | tf_op jit(solution)/shard_map/reduce_scatter | solution.py:67
  32.5 218.3 %copy-start.7 = (f32[1000]{0:T(1024)S(1)}, f32[1000]{0:T(1024)}, u32[]{:S(2)}) copy-start(f32[1000]{0:T(1024)} %param.20) | copy-start | bytes 12004
  32.5 218.9 %copy-start.9 = (f32[1000]{0:T(1024)S(1)}, f32[1000]{0:T(1024)}, u32[]{:S(2)}) copy-start(f32[1000]{0:T(1024)} %param.21) | copy-start | bytes 12004
  32.5 492.7 %all-gather.4.cloned.1.call-start = ((), (), s32[]{:S(2)}) async-start(), calls=%async_computation.5 | async-start | bytes 11206656 | tf_op jit(solution)/shard_map/all_gather | solution.py:74
  251.4 16.1 copy-start.4
  435.5 128.5 %reduce-scatter.7.cloned.1.call-start = ((), (), s32[]{:S(2)}) async-start(), calls=%async_computation.6 | async-start | bytes 22413312 | tf_op jit(solution)/shard_map/reduce_scatter | solution.py:78
  539.6 440.7 %all-gather.6.cloned.1.call-start = ((), (), s32[]{:S(2)}) async-start(), calls=%async_computation.7 | async-start | bytes 11206656 | tf_op jit(solution)/shard_map/all_gather | solution.py:110
  539.6 62.8 %copy-start.6 = (f32[1000]{0:T(1024)S(1)}, f32[1000]{0:T(1024)}, u32[]{:S(2)}) copy-start(f32[1000]{0:T(1024)} %param.24) | copy-start | bytes 12004
  539.6 62.8 %copy-start.8 = (f32[1000]{0:T(1024)S(1)}, f32[1000]{0:T(1024)}, u32[]{:S(2)}) copy-start(f32[1000]{0:T(1024)} %param.25) | copy-start | bytes 12004
  602.5 16.1 copy-start.3
  778.2 9.6 slice-start
  778.2 9.6 slice-start.1
  944.0 14.1 copy-start.11
  944.0 14.1 copy-start.13
  964.4 201.5 %reduce-scatter.9.cloned.1.call-start = ((), (), s32[]{:S(2)}) async-start(), calls=%async_computation.8 | async-start | bytes 22413312 | tf_op jit(solution)/shard_map/reduce_scatter | solution.py:117
  994.7 453.4 %all-gather.8.cloned.1.call-start = ((), (), s32[]{:S(2)}) async-start(), calls=%async_computation.9 | async-start | bytes 11206656 | tf_op jit(solution)/shard_map/all_gather | solution.py:138
  999.6 4.5 copy-start.2
  1246.9 91.2 %copy-start.10 = (f32[1000]{0:T(1024)S(1)}, f32[1000]{0:T(1024)}, u32[]{:S(2)}) copy-start(f32[1000]{0:T(1024)} %get-tuple-element.530) | copy-start | bytes 12004
  1338.0 14.0 copy-start.12
  1338.0 14.0 copy-start.14
  1358.4 370.2 %all-reduce.9.cloned.1.call-start = ((), (), s32[]{:S(2)}) async-start(), calls=%async_computation.11 | async-start | bytes 16384000 | tf_op jit(solution)/shard_map/psum | solution.py:146
  1374.0 88.7 %copy-start.15 = (bf16[1000,1000]{1,0:T(8,128)(2,1)S(1)}, bf16[1000,1000]{1,0:T(8,128)(2,1)}, u32[]{:S(2)}) copy-start(bf16[1000,1000]{1,0:T(8,128)(2,1)} %param.19) | copy-start | bytes 6000004
  1462.7 291.7 %reduce-scatter.11.cloned.1.call-start = ((), (), s32[]{:S(2)}) async-start(), calls=%async_computation.10 | async-start | bytes 22413312 | tf_op jit(solution)/shard_map/reduce_scatter | solution.py:145
  1728.6 37.2 %copy-start.1 = (bf16[1000,1000]{1,0:T(8,128)(2,1)S(1)}, bf16[1000,1000]{1,0:T(8,128)(2,1)}, u32[]{:S(2)}) copy-start(bf16[1000,1000]{1,0:T(8,128)(2,1)} %param.23) | copy-start | bytes 6000004
  1754.3 9.4 copy-start.5
Sparse Core Ops, SparseCore 0:
  32.6 172.5 reduce-scatter.4
  435.6 89.5 all-gather.3
  539.7 24.3 reduce-scatter.6
  964.5 15.7 all-gather.5
  994.9 171.0 reduce-scatter.8
  1358.5 89.5 all-gather.7
  1462.8 265.7 all-reduce.8
  1731.0 23.3 reduce-scatter.10
where the time goes:
time: 1800 us; the launch traced here: 1770 us
  waiting for transfers between devices  764 us (42%)
  other arithmetic  495 us (28%)
  blocking collectives  210 us (12%)
  local copies, waits for them, and re-layouts  188 us (10%)
  matrix products  98.8 us (5%)
    while x300, other arithmetic  286 us
    psum x1, waiting for transfers between devices, on_device(): lax.psum((weight_grad_second, weight_grad_third), 'dp')  227 us
    reduce_scatter x1, waiting for transfers between devices, on_device(): lax.psum_scatter(partial_second, 'row', scatter_dimension=1, tiled=True)  173 us
    reduce_scatter x1, waiting for transfers between devices, on_device(): lax.psum_scatter(partial_hidden, 'row', scatter_dimension=1, tiled=True)  149 us
    dynamic_update_slice x120, local copies, waits for them, and re-layouts, run_recurrence(): _, states = lax.scan(advance, start, pre_norm, unroll=5)  91.4 us
    all_gather x1, waiting for transfers between devices, on_device(): hidden_full = lax.all_gather(hidden_low, 'row', axis=1, tiled=True)  89.2 us
    psum x1, blocking collectives, on_device(): lax.psum((jnp.sum(norm_grad_second * unit_second, axis=(0, 1)), jnp.sum(n...  75.9 us
    all_gather x1, waiting for transfers between devices, on_device(): lax.all_gather(proj_grad_second, 'row', axis=1, tiled=True)  74 us
  transfers between devices with their start and end apart: 8, of which 8 were waited for; matrix products, arithmetic and copies ran while one was open for 5% of the time, Pallas kernels for 0%

commit v1 on v0

v1 whole, which is shorter than its diff:
```python
import functools

import jax
import jax.numpy as jnp
from jax import lax
from jax.experimental import pallas as pl
from jax.experimental.pallas import tpu as pltpu
from jax.sharding import PartitionSpec as P

norm_eps = 1e-05
gelu_outer = 0.7978845608028654
gelu_inner = gelu_outer * 0.044715
LANES = 128
BLOCK = 256
f32 = jnp.float32
bf16 = jnp.bfloat16


def params():
    return pltpu.CompilerParams(vmem_limit_bytes=56 * 2**20)


def round_up(value, unit):
    return -(-value // unit) * unit


def whole(shape):
    return pl.BlockSpec(shape, lambda *_: (0,) * len(shape), pipeline_mode=pl.Buffered(1))


def dot(left, right, dims):
    return lax.dot_general(left, right, (dims, ((), ())), preferred_element_type=f32)


def tie(value, after):
    return lax.optimization_barrier((value, after))[0]


def tile_of(j):
    return pl.ds(j * LANES, LANES)


def held(j, low, count):
    return jnp.clip(j - low, 0, count - 1)


def prep_kernel(seqs, pitch, width, base, at_ref, inputs, *refs):
    near, send, scratch, packed = refs[-4:]
    steps, group, block = inputs.shape
    lane = base + pl.program_id(0) * block + lax.broadcasted_iota(jnp.int32, (1, LANES), 1)
    rows = near.shape[0]
    for k in range(block // LANES):
        scratch[...] = inputs[:, :, tile_of(k)].astype(f32).reshape(steps * group, LANES)
        for place, out in ((0, near), (1, send)):
            first = at_ref[place]
            for s in range(seqs):
                packed[s * pitch : s * pitch + steps, :] = scratch[pl.ds(first + s, steps, stride=group), :]
                packed[s * pitch + steps : (s + 1) * pitch, :] = jnp.zeros((pitch - steps, LANES), f32)
            out[:, tile_of(k)] = jnp.where(lane + k * LANES < width, packed[...], 0.0).astype(bf16)


def prep(inputs, places, seqs, pitch, half, first, blocks, near=None):
    steps, group, width = inputs.shape
    rows = seqs * pitch
    near_spec = pl.BlockSpec((rows, BLOCK), lambda j, at: (0, j + first))
    return pl.pallas_call(
        functools.partial(prep_kernel, seqs, pitch, width, first * BLOCK),
        grid_spec=pltpu.PrefetchScalarGridSpec(
            num_scalar_prefetch=1,
            grid=(blocks,),
            in_specs=[pl.BlockSpec((steps, group, BLOCK), lambda j, at: (0, 0, j + first))]
            + ([] if near is None else [pl.BlockSpec(memory_space=pl.ANY)]),
            out_specs=[near_spec, pl.BlockSpec((rows, BLOCK), lambda j, at: (0, j))],
            scratch_shapes=[pltpu.VMEM((steps * group, LANES), f32), pltpu.VMEM((rows, LANES), f32)],
        ),
        out_shape=[
            jax.ShapeDtypeStruct((rows, half), bf16),
            jax.ShapeDtypeStruct((rows, blocks * BLOCK), bf16),
        ],
        input_output_aliases={} if near is None else {2: 0},
        compiler_params=params(),
        name="prep",
    )(places, inputs, *(() if near is None else (near,)))


def prep_grads_kernel(pitch, width, at_ref, own, other, near, send, packed):
    seqs, steps, block = own.shape
    lane = pl.program_id(0) * block + lax.broadcasted_iota(jnp.int32, (1, block), 1)
    for part, out in ((own, near), (other, send)):
        for s in range(seqs):
            packed[s * pitch : s * pitch + steps, :] = part[s].astype(f32)
            packed[s * pitch + steps : (s + 1) * pitch, :] = jnp.zeros((pitch - steps, block), f32)
        out[...] = jnp.where(lane < width, packed[...], 0.0).astype(bf16)


def prep_grads(grads, places, seqs, pitch, half):
    _, steps, width = grads.shape
    rows = seqs * pitch
    out = pl.BlockSpec((rows, BLOCK), lambda j, at: (0, j))
    return pl.pallas_call(
        functools.partial(prep_grads_kernel, pitch, width),
        grid_spec=pltpu.PrefetchScalarGridSpec(
            num_scalar_prefetch=1,
            grid=(half // BLOCK,),
            in_specs=[
                pl.BlockSpec((seqs, steps, BLOCK), lambda j, at: (at[0], 0, j)),
                pl.BlockSpec((seqs, steps, BLOCK), lambda j, at: (at[1], 0, j)),
            ],
            out_specs=[out, out],
            scratch_shapes=[pltpu.VMEM((rows, BLOCK), f32)],
        ),
        out_shape=[jax.ShapeDtypeStruct((rows, half), bf16)] * 2,
        compiler_params=params(),
        name="prep_grads",
    )(places, grads, grads)


def combine_kernel(pitch, at_ref, a_near, b_near, a_far0, a_far1, b_far, out):
    seqs, steps, block = out.shape

    def put(a, b):
        total = a[...].astype(f32) + b[...].astype(f32)
        for s in range(seqs):
            out[s] = total[s * pitch : s * pitch + steps, :]

    part, lanes = pl.program_id(0), pl.program_id(1)
    cut = pl.num_programs(1) // 2
    pl.when(part == 0)(lambda: put(a_near, b_near))
    pl.when((part == 1) & (lanes < cut))(lambda: put(a_far0, b_far))
    pl.when((part == 1) & (lanes >= cut))(lambda: put(a_far1, b_far))


def combine(places, a_near, b_near, a_far, b_far, seqs, steps, width):
    rows, half = a_near.shape
    nb = half // BLOCK
    far0, far1 = a_far
    cut = far0.shape[1] // BLOCK if len(a_far) > 1 else nb
    near_spec = pl.BlockSpec((rows, BLOCK), lambda p, j, at: (0, jnp.where(p == 0, j, nb - 1)))
    far_spec = pl.BlockSpec((rows, BLOCK), lambda p, j, at: (0, jnp.where(p == 0, 0, j)))
    split = far0.shape[1] < half
    far0_spec = pl.BlockSpec((rows, BLOCK), lambda p, j, at: (0, jnp.where(p == 0, 0, jnp.minimum(j, nb // 2 - 1))))
    far1_at = 0 if split else nb // 2
    far1_spec = pl.BlockSpec(
        (rows, BLOCK), lambda p, j, at: (0, far1_at + jnp.where(p == 0, 0, jnp.maximum(j - nb // 2, 0)))
    )
    return pl.pallas_call(
        functools.partial(combine_kernel, rows // seqs),
        grid_spec=pltpu.PrefetchScalarGridSpec(
            num_scalar_prefetch=1,
            grid=(2, nb),
            in_specs=[near_spec, near_spec, far0_spec, far1_spec, far_spec],
            out_specs=pl.BlockSpec((seqs, steps, BLOCK), lambda p, j, at: (at[p], 0, j)),
        ),
        out_shape=jax.ShapeDtypeStruct((2 * seqs, steps, width), f32),
        compiler_params=params(),
        name="combine",
    )(places, a_near, b_near, far0, far1, b_far)


def cut_kernel(pieces, at_ref, weight, out):
    tall, wide = out.shape
    start = (pl.program_id(0) * pieces + at_ref[0]) * tall
    row = start + lax.broadcasted_iota(jnp.int32, (tall, wide), 0)
    lane = lax.broadcasted_iota(jnp.int32, (tall, wide), 1)
    limit_rows, limit_lanes = at_ref[1], at_ref[2]
    value = weight[...].astype(f32)
    out[...] = jnp.where((row < limit_rows) & (lane < limit_lanes), value, 0.0).astype(bf16)


def cut(weight, place, chunks, pieces, half):
    tall = half // (chunks * pieces)
    at = jnp.stack([place, jnp.int32(weight.shape[0]), jnp.int32(weight.shape[1])]).astype(jnp.int32)
    return pl.pallas_call(
        functools.partial(cut_kernel, pieces),
        grid_spec=pltpu.PrefetchScalarGridSpec(
            num_scalar_prefetch=1,
            grid=(chunks,),
            in_specs=[pl.BlockSpec((tall, half), lambda j, at: (j * pieces + at[0], 0))],
            out_specs=pl.BlockSpec((tall, half), lambda j, at: (j, 0)),
        ),
        out_shape=jax.ShapeDtypeStruct((chunks * tall, half), bf16),
        compiler_params=params(),
        name="cut",
    )(at, weight)


def project_kernel(parts, halves, add, nb, *refs):
    xs = refs[:parts]
    ws = [refs[parts * (1 + h) : parts * (2 + h)] for h in range(halves)]
    refs = refs[parts * (1 + halves) :]
    proj, sums = refs[-2:]
    j = pl.program_id(0)

    def go(weights):
        acc = sum(dot(x[...], w[...], ((1,), (0,))) for x, w in zip(xs, weights))
        if add:
            acc = acc + jnp.concatenate([refs[0][k] for k in range(BLOCK // LANES)], axis=1)
        for k in range(BLOCK // LANES):
            proj[k] = acc[:, k * LANES : (k + 1) * LANES]
        sums[0:1, :] = jnp.sum(acc, axis=0, keepdims=True)
        sums[1:2, :] = jnp.sum(acc * acc, axis=0, keepdims=True)

    for h in range(halves):
        pl.when((j >= h * nb) & (j < (h + 1) * nb))(functools.partial(go, ws[h]))


def project(xs, ws, tiles, first=0, before=None, add=False):
    rows = xs[0][0].shape[0]
    half = ws[0][0].shape[1]
    nb = half // BLOCK
    specs, operands = [], []
    for x, at, depth in xs:
        specs.append(pl.BlockSpec((rows, depth), lambda j, at=at: (0, at), pipeline_mode=pl.Buffered(1)))
        operands.append(x)
    for h, weights in enumerate(ws):
        for w, (_, _, depth) in zip(weights, xs):
            specs.append(pl.BlockSpec((depth, BLOCK), lambda j, h=h: (0, held(j, h * nb, nb))))
            operands.append(w)
    tile_spec = pl.BlockSpec((BLOCK // LANES, rows, LANES), lambda j: (j + first, 0, 0))
    aliases = {}
    if before is not None:
        aliases = {len(operands): 0}
        operands.append(before)
        specs.append(tile_spec if add else pl.BlockSpec(memory_space=pl.ANY))
    width = len(ws) * half
    return pl.pallas_call(
        functools.partial(project_kernel, len(xs), len(ws), add, nb),
        grid=(len(ws) * nb,),
        in_specs=specs,
        out_specs=[tile_spec, pl.BlockSpec((2, BLOCK), lambda j: (0, j))],
        out_shape=[
            jax.ShapeDtypeStruct((tiles, rows, LANES), f32),
            jax.ShapeDtypeStruct((2, width), f32),
        ],
        input_output_aliases=aliases,
        compiler_params=params(),
        name="project",
    )(*operands)


def stats_of(sums, gains, count, j):
    mean = sums[0:1, tile_of(j)] / count
    var = sums[1:2, tile_of(j)] / count - mean * mean
    scale = lax.rsqrt(var + norm_eps)
    return mean, scale


def clear_pads(steps, seqs, array):
    tiles, rows, _ = array.shape
    pitch = rows // seqs
    if pitch > steps:
        for j in range(tiles):
            for s in range(seqs):
                array[j, s * pitch + steps : (s + 1) * pitch, :] = jnp.zeros((pitch - steps, LANES), f32)


def run_forward(steps, seqs, tiles, norm, gains, states, slopes):
    recur = [jnp.broadcast_to(gains[2:3, tile_of(j)], (seqs, LANES)) for j in range(tiles)]
    pitch = norm.shape[1] // seqs

    def advance(t, before):
        now = []
        at = pl.ds(t, seqs, stride=pitch)
        for j in range(tiles):
            arg = norm[j, at, :] + recur[j] * before[j]
            poly = gelu_inner * (arg * arg) + gelu_outer
            tanh = jnp.tanh(arg * poly)
            half = 0.5 * arg
            state = half + half * tanh
            states[j, at, :] = state
            inner = 3.0 * poly - 2.0 * gelu_outer
            slopes[j, at, :] = (0.5 * tanh + 0.5) + half * (1.0 - tanh * tanh) * inner
            now.append(state)
        return tuple(now)

    unroll = 2 if steps % 2 == 0 else 1

    def several(i, before):
        for k in range(unroll):
            before = advance(i * unroll + k, before)
        return before

    zero = jnp.zeros((seqs, LANES), f32)
    lax.fori_loop(0, steps // unroll, several, (zero,) * tiles)
    clear_pads(steps, seqs, states)


def run_backward(steps, seqs, tiles, grads, gains, slopes, arg_grads):
    recur = [jnp.broadcast_to(gains[2:3, tile_of(j)], (seqs, LANES)) for j in range(tiles)]
    pitch = arg_grads.shape[1] // seqs

    def retreat(t, after):
        now = []
        at = pl.ds(t, seqs, stride=pitch)
        for j in range(tiles):
            grad = (grads[j, at, :] + recur[j] * after[j]) * slopes[j, at, :]
            arg_grads[j, at, :] = grad
            now.append(grad)
        return tuple(now)

    unroll = 2 if steps % 2 == 0 else 1

    def several(i, after):
        for k in range(unroll):
            after = retreat(steps - 1 - (i * unroll + k), after)
        return after

    zero = jnp.zeros((seqs, LANES), f32)
    lax.fori_loop(0, steps // unroll, several, (zero,) * tiles)
    clear_pads(steps, seqs, arg_grads)


def back_sums(tiles, arg_grads, proj, states, sums, gains, count, out):
    rows = proj.shape[1]
    for j in range(tiles):
        mean, scale = stats_of(sums, gains, count, j)
        grad = arg_grads[j]
        out[0:1, tile_of(j)] = scale * jnp.sum(grad * (proj[j] - mean), axis=0, keepdims=True)
        out[1:2, tile_of(j)] = jnp.sum(grad, axis=0, keepdims=True)
        out[2:3, tile_of(j)] = jnp.sum(
            arg_grads[j, 1:rows, :] * states[j, 0 : rows - 1, :], axis=0, keepdims=True
        )


def make_norm(tiles, proj, sums, gains, count, norm):
    for j in range(tiles):
        mean, scale = stats_of(sums, gains, count, j)
        norm[j] = (proj[j] - mean) * (gains[0:1, tile_of(j)] * scale) + gains[1:2, tile_of(j)]


def first_layer_kernel(steps, seqs, count, proj, sums, gains, hidden, slopes, totals, norm, states):
    tiles = proj.shape[0]
    make_norm(tiles, proj, sums, gains, count, norm)
    run_forward(steps, seqs, tiles, norm, gains, states, slopes)
    for j in range(tiles):
        hidden[:, tile_of(j)] = states[j].astype(bf16)
        totals[0:1, tile_of(j)] = jnp.sum(states[j], axis=0, keepdims=True)


def first_layer(steps, seqs, count, proj, sums, gains):
    tiles, rows, _ = proj.shape
    return pl.pallas_call(
        functools.partial(first_layer_kernel, steps, seqs, count),
        out_shape=[
            jax.ShapeDtypeStruct((rows, tiles * LANES), bf16),
            jax.ShapeDtypeStruct((tiles, rows, LANES), f32),
            jax.ShapeDtypeStruct((1, tiles * LANES), f32),
        ],
        scratch_shapes=[pltpu.VMEM((tiles, rows, LANES), f32)] * 2,
        compiler_params=params(),
        name="first_layer",
    )(proj, sums, gains)


def second_layer_kernel(
    steps, seqs, count, proj, sums, gains, cot_near, cot_far, near, far, arg_grads, out, norm, states, slopes
):
    tiles = proj.shape[0]
    make_norm(tiles, proj, sums, gains, count, norm)
    run_forward(steps, seqs, tiles, norm, gains, states, slopes)
    half = tiles // 2
    for j in range(half):
        near[:, tile_of(j)] = states[j]
        far[:, tile_of(j)] = states[half + j].astype(bf16)
        norm[j] = cot_near[:, tile_of(j)].astype(f32)
        norm[half + j] = cot_far[:, tile_of(j)].astype(f32)
    run_backward(steps, seqs, tiles, norm, gains, slopes, arg_grads)
    back_sums(tiles, arg_grads, proj, states, sums, gains, count, out)


def second_layer(steps, seqs, count, proj, sums, gains, cot_near, cot_far):
    tiles, rows, _ = proj.shape
    width = tiles * LANES
    return pl.pallas_call(
        functools.partial(second_layer_kernel, steps, seqs, count),
        out_shape=[
            jax.ShapeDtypeStruct((rows, width // 2), f32),
            jax.ShapeDtypeStruct((rows, width // 2), bf16),
            jax.ShapeDtypeStruct((tiles, rows, LANES), f32),
            jax.ShapeDtypeStruct((3, width), f32),
        ],
        scratch_shapes=[pltpu.VMEM((tiles, rows, LANES), f32)] * 3,
        compiler_params=params(),
        name="second_layer",
    )(proj, sums, gains, cot_near, cot_far)


def norm_back(steps, pitch, arg_grads, proj, sums, gains, totals, count, out, columns):
    tiles, rows, _ = proj.shape
    row = lax.broadcasted_iota(jnp.int32, (rows, LANES), 0)
    inside = lax.rem(row, pitch) < steps
    for j in range(tiles):
        mean, scale = stats_of(sums, gains, count, j)
        factor = gains[0:1, tile_of(j)] * scale
        shift_part = totals[1:2, tile_of(j)] / count
        unit_part = scale * totals[0:1, tile_of(j)] / count
        grad = factor * (arg_grads[j] - shift_part - (proj[j] - mean) * unit_part)
        low = jnp.where(inside, grad, 0.0).astype(bf16).astype(f32)
        column = jnp.sum(low, axis=0, keepdims=True)
        high_part = column.astype(bf16).astype(f32)
        low_part = (column - high_part).astype(bf16).astype(f32)
        columns[0:1, tile_of(j)] = high_part + low_part
        low = jnp.where(row == steps, high_part, jnp.where(row == steps + 1, low_part, low))
        out[:, tile_of(j)] = low.astype(bf16)


def pull_kernel(steps, pitch, count, nb, tiled, arg_grads, proj, sums, gains, totals, w_nn, w_nf, w_fn, w_ff, low, columns, *outs):
    j = pl.program_id(0)
    half = w_nn.shape[1]

    @pl.when(j == 0)
    def _():
        norm_back(steps, pitch, arg_grads, proj, sums, gains, totals, count, low, columns)

    def go(left, right):
        return dot(low[:, :half], left[...], ((1,), (1,))) + dot(low[:, half:], right[...], ((1,), (1,)))

    if tiled:
        (out,) = outs

        def put(acc):
            for k in range(BLOCK // LANES):
                out[k] = acc[:, k * LANES : (k + 1) * LANES]

        pl.when(j < nb)(lambda: put(go(w_nn, w_nf)))
        pl.when(j >= nb)(lambda: put(go(w_fn, w_ff)))
    else:
        near, far = outs

        @pl.when(j < nb)
        def _():
            far[...] = go(w_fn, w_ff).astype(bf16)

        @pl.when(j >= nb)
        def _():
            near[...] = go(w_nn, w_nf)


def pull(steps, seqs, count, arg_grads, proj, sums, gains, totals, quarters, tiled):
    tiles, rows, _ = proj.shape
    width = tiles * LANES
    half = width // 2
    nb = half // BLOCK
    near_low, far_low = (0, nb) if tiled else (nb, 0)
    near_spec = pl.BlockSpec((BLOCK, half), lambda j: (held(j, near_low, nb), 0))
    far_spec = pl.BlockSpec((BLOCK, half), lambda j: (held(j, far_low, nb), 0))
    specs = [pl.BlockSpec((rows, width), lambda j: (0, 0)), pl.BlockSpec((1, width), lambda j: (0, 0))]
    shapes = [jax.ShapeDtypeStruct((rows, width), bf16), jax.ShapeDtypeStruct((1, width), f32)]
    if tiled:
        specs += [pl.BlockSpec((BLOCK // LANES, rows, LANES), lambda j: (j, 0, 0))]
        shapes += [jax.ShapeDtypeStruct((tiles, rows, LANES), f32)]
    else:
        specs += [
            pl.BlockSpec((rows, BLOCK), lambda j: (0, held(j, near_low, nb))),
            pl.BlockSpec((rows, BLOCK), lambda j: (0, held(j, far_low, nb))),
        ]
        shapes += [jax.ShapeDtypeStruct((rows, half), f32), jax.ShapeDtypeStruct((rows, half), bf16)]
    return pl.pallas_call(
        functools.partial(pull_kernel, steps, rows // seqs, count, nb, tiled),
        grid=(2 * nb,),
        in_specs=[
            whole((tiles, rows, LANES)),
            whole((tiles, rows, LANES)),
            whole((2, width)),
            whole((3, width)),
            whole((3, width)),
            near_spec,
            near_spec,
            far_spec,
            far_spec,
        ],
        out_specs=specs,
        out_shape=shapes,
        compiler_params=params(),
        name="pull",
    )(arg_grads, proj, sums, gains, totals, *quarters)


def first_back_kernel(steps, seqs, count, grads, slopes, hidden, proj, sums, gains, arg_grads, out, states):
    tiles = proj.shape[0]
    run_backward(steps, seqs, tiles, grads, gains, slopes, arg_grads)
    for j in range(tiles):
        states[j] = hidden[:, tile_of(j)].astype(f32)
    back_sums(tiles, arg_grads, proj, states, sums, gains, count, out)


def first_back(steps, seqs, count, grads, slopes, hidden, proj, sums, gains):
    tiles, rows, _ = proj.shape
    return pl.pallas_call(
        functools.partial(first_back_kernel, steps, seqs, count),
        out_shape=[
            jax.ShapeDtypeStruct((tiles, rows, LANES), f32),
            jax.ShapeDtypeStruct((3, tiles * LANES), f32),
        ],
        scratch_shapes=[pltpu.VMEM((tiles, rows, LANES), f32)],
        compiler_params=params(),
        name="first_back",
    )(grads, slopes, hidden, proj, sums, gains)


def weight_kernel(steps, parts, centred, *refs):
    xs, refs = refs[: len(parts)], refs[len(parts) :]
    if centred:
        centre, *refs = refs
    low, q_nn, q_nf, q_fn, q_ff = refs
    half = low.shape[1] // 2
    j = pl.program_id(0)
    total = sum(parts)

    def go(x, left, right):
        value = x[...]
        if centred:
            row = lax.broadcasted_iota(jnp.int32, value.shape, 0)
            minus = jnp.broadcast_to(-centre[...], value.shape)
            value = jnp.where((row == steps) | (row == steps + 1), minus, value.astype(f32)).astype(bf16)
        acc = dot(value, low[...], ((0,), (0,)))
        left[...] = acc[:, :half].astype(left.dtype)
        right[...] = acc[:, half:].astype(right.dtype)

    start = 0
    for x, blocks in zip(xs, parts):
        outs = (q_nn, q_nf) if start < total // 2 else (q_fn, q_ff)
        pl.when((j >= start) & (j < start + blocks))(functools.partial(go, x, *outs))
        start += blocks


def weight_grad(steps, xs, low, centre=None):
    rows, width = low.shape
    half = width // 2
    nb = half // BLOCK
    specs, start = [], 0
    for _, first, blocks in xs:
        specs.append(
            pl.BlockSpec((rows, BLOCK), lambda j, start=start, first=first, blocks=blocks: (0, first + held(j, start, blocks)))
        )
        start += blocks
    operands = [x for x, _, _ in xs]
    if centre is not None:
        specs.append(pl.BlockSpec((1, BLOCK), lambda j: (0, j)))
        operands.append(centre)
    first = pl.BlockSpec((BLOCK, half), lambda j: (held(j, 0, nb), 0))
    second = pl.BlockSpec((BLOCK, half), lambda j: (held(j, nb, nb), 0))
    return pl.pallas_call(
        functools.partial(weight_kernel, steps, [b for _, _, b in xs], centre is not None),
        grid=(2 * nb,),
        in_specs=specs + [whole((rows, width))],
        out_specs=[first, first, second, second],
        out_shape=[jax.ShapeDtypeStruct((half, half), bf16)] * 4,
        compiler_params=params(),
        name="weight_grad",
    )(*operands, low)


def over(value, axis):
    return lax.ppermute(value, axis, [(0, 1), (1, 0)])


def across(value, bit):
    size = lax.axis_size("dp")
    return lax.ppermute(value, "dp", [(i, i ^ bit) for i in range(size)])


def dp_bits():
    return [1 << k for k in range((lax.axis_size("dp") - 1).bit_length())]


def swap_halves(value):
    half = value.shape[-1] // 2
    return jnp.concatenate([value[:, half:], value[:, :half]], axis=1)


def sum_step(value, step, swaps):
    if step not in ("col", "row"):
        return value + across(value, step)
    other = over(value, step)
    rows = [swap_halves(other[k : k + 1]) if axis == step else other[k : k + 1] for k, axis in enumerate(swaps)]
    return value + jnp.concatenate(rows, axis=0)


def join(place, bit, own, other):
    mine = (place // bit) % 2
    return jnp.where(mine == 0, jnp.concatenate([own, other], axis=0), jnp.concatenate([other, own], axis=0))


def gather_dp(piece, bits):
    place = lax.axis_index("dp")
    for bit in bits:
        piece = join(place, bit, piece, across(piece, bit))
    return piece


def halve_dp(total, bit):
    mine = (lax.axis_index("dp") // bit) % 2
    half = total.shape[0] // 2
    kept = lax.dynamic_slice_in_dim(total, mine * half, half, 0)
    sent = lax.dynamic_slice_in_dim(total, (1 - mine) * half, half, 0)
    return kept + across(sent.astype(bf16), bit).astype(f32)


def reduce_row_first(own, other):
    total = own + over(other.astype(bf16), "row").astype(f32)
    for bit in dp_bits():
        total = halve_dp(total, bit)
    return gather_dp(total.astype(bf16), reversed(dp_bits()))


def reduce_row_last(own, other):
    for bit in dp_bits():
        own, other = halve_dp(own, bit), halve_dp(other, bit)
    total = own + over(other.astype(bf16), "row").astype(f32)
    return gather_dp(total.astype(bf16), reversed(dp_bits()))


def on_device(
    inputs,
    w_second,
    gain_second,
    shift_second,
    recur_second,
    w_third,
    gain_third,
    shift_third,
    recur_third,
    cotangent,
):
    steps, seq_group, width = inputs.shape
    share = cotangent.shape[1]
    seqs = share // lax.axis_size("row")
    pitch = round_up(steps + 2, 8)
    rows = seqs * pitch
    half = round_up(width, 2 * BLOCK)
    nb = half // BLOCK
    tiles = 2 * half // LANES
    pieces = lax.axis_size("dp")
    count = steps * seq_group * pieces
    row, col, place = lax.axis_index("row"), lax.axis_index("col"), lax.axis_index("dp")
    bits = dp_bits()
    turned = sum(((place // bit) % 2) * (pieces // 2 // bit) for bit in bits)

    def pad_weight(w):
        return jnp.pad(w, ((0, half - w.shape[0]), (0, half - w.shape[1])))

    def pad_params(*vectors):
        return jnp.pad(jnp.stack(vectors), ((0, 0), (0, half - width)))

    chunks = 2
    spread = half // (chunks * pieces) >= 16
    if spread:
        cut_second = cut(w_second, turned, chunks, pieces, half)
        cut_third = cut(w_third, turned, 1, pieces, half)
        tall = half // (chunks * pieces)
        far_second = [over(cut_second[k * tall : (k + 1) * tall], "row") for k in range(chunks)]
        far_third = over(cut_third, "row")

    places = jnp.stack([col * share + row * seqs, col * share + (1 - row) * seqs]).astype(jnp.int32)
    parts = jnp.stack([row, 1 - row]).astype(jnp.int32)
    x_near, send0 = prep(inputs, places, seqs, pitch, half, 0, nb // 2)
    x_far0 = over(send0, "row")
    x_near, send1 = prep(inputs, places, seqs, pitch, half, nb // 2, nb // 2, x_near)
    x_far1 = over(send1, "row")

    nn2 = pad_weight(w_second)
    nf2 = over(nn2, "col")
    own_second = pad_params(gain_second, shift_second, recur_second)
    own_third = pad_params(gain_third, shift_third, recur_third)
    gains_second = jnp.concatenate([own_second, over(own_second, "col")], axis=1)
    nn3 = pad_weight(w_third)
    fn3 = over(nn3, "col")
    if spread:
        fn2 = [gather_dp(piece, reversed(bits)) for piece in far_second]
        nf3 = gather_dp(far_third, reversed(bits[1:]))
    else:
        far = over(nn2, "row")
        fn2 = [far[: half // 2], far[half // 2 :]]
        nf3 = over(nn3, "row")
    ff2 = [over(chunk, "col") for chunk in fn2]

    proj_second, _ = project([(x_near, 0, half)], [[nn2], [nf2]], tiles)
    proj_second, _ = project([(x_far0, 0, half // 2)], [[fn2[0]], [ff2[0]]], tiles, 0, proj_second, True)
    proj_second, sums = project([(x_far1, 0, half // 2)], [[fn2[1]], [ff2[1]]], tiles, 0, proj_second, True)

    swaps = ("col", "col")
    sums = sum_step(sums, "col", swaps)
    sums = sum_step(sums, "row", swaps)
    grads = tie(jnp.transpose(cotangent, (1, 0, 2)), sums)
    cot_near, cot_send = prep_grads(grads, parts, seqs, pitch, half)
    cot_far = over(cot_send, "row")
    sums = sum_step(sums, bits[0], swaps) if bits else sums
    if spread and bits:
        nf3 = gather_dp(tie(nf3, sums), bits[:1])
    for bit in bits[1:]:
        sums = sum_step(sums, bit, swaps)
    sums_second = sums
    ff3 = over(nf3, "col")
    gains_third = jnp.concatenate([own_third, over(own_third, "row")], axis=1)
    hidden, slopes_second, hidden_sums = first_layer(steps, seqs, count, proj_second, sums_second, gains_second)
    hidden_parts = [(hidden, 0, half), (hidden, 1, half)]
    proj_third, sums_near = project(hidden_parts, [[nn3, fn3]], tiles)
    proj_third, sums_far = project(hidden_parts, [[nf3, ff3]], tiles, nb, proj_third)

    swaps = ("row", "row", "col")
    sums = jnp.concatenate([jnp.concatenate([sums_near, sums_far], axis=1), hidden_sums], axis=0)
    for step in ("col", *bits, "row"):
        sums = sum_step(sums, step, swaps)
    sums_third, centre = sums[:2], (sums[2:3] / count).astype(bf16).astype(f32)
    states_near, states_far, arg_grads_third, sums = second_layer(
        steps, seqs, count, proj_third, sums_third, gains_third, cot_near, cot_far
    )
    swaps = ("row", "row", "row")
    sums = sum_step(sums, "col", swaps)
    sums = sum_step(sums, "row", swaps)
    states_far = over(tie(states_far, sums), "row")
    for bit in bits:
        sums = sum_step(sums, bit, swaps)
    totals_third = sums
    low_third, columns, grad_hidden = pull(
        steps, seqs, count, arg_grads_third, proj_third, sums_third, gains_third, totals_third, [nn3, nf3, fn3, ff3], True
    )
    nn, nf, fn, ff = weight_grad(steps, [(hidden, 0, nb), (hidden, nb, nb)], low_third, centre)
    own3 = nn.astype(f32) + over(fn, "col").astype(f32)
    other3 = nf.astype(f32) + over(ff, "col").astype(f32)
    arg_grads_second, sums = first_back(
        steps, seqs, count, grad_hidden, slopes_second, hidden, proj_second, sums_second, gains_second
    )
    swaps = ("col", "col", "col", "row")
    sums = jnp.concatenate([sums, columns], axis=0)
    for step in ("col", *bits, "row"):
        sums = sum_step(sums, step, swaps)
    totals_second, columns = sums[:3], sums[3:4]
    grad_w_third = reduce_row_last(tie(own3, sums), tie(other3, sums))
    low_second, _, grad_near, grad_far = pull(
        steps,
        seqs,
        count,
        arg_grads_second,
        proj_second,
        sums_second,
        gains_second,
        totals_second,
        [nn2, nf2, jnp.concatenate(fn2, axis=0), jnp.concatenate(ff2, axis=0)],
        False,
    )
    grad_far = over(grad_far, "row")
    nn, nf, fn, ff = weight_grad(
        steps, [(x_near, 0, nb), (x_far0, 0, nb // 2), (x_far1, 0, nb // 2)], low_second
    )
    own2 = nn.astype(f32) + over(nf, "col").astype(f32)
    other2 = fn.astype(f32) + over(ff, "col").astype(f32)
    grad_w_second = reduce_row_last(own2, other2)

    output = combine(parts, x_near, states_near, (send0, send1), states_far, seqs, steps, width)
    grad_inputs = combine(parts, cot_near, grad_near, (cot_send, cot_send), grad_far, seqs, steps, width)
    output = jnp.transpose(output, (1, 0, 2))
    grad_inputs = jnp.transpose(grad_inputs, (1, 0, 2))
    restore = centre[0, :width, None] * columns[0, None, :width]
    return (
        output,
        grad_inputs,
        grad_w_second[:width, :width].astype(f32),
        totals_second[0, :width],
        totals_second[1, :width],
        totals_second[2, :width],
        grad_w_third[:width, :width].astype(f32) + restore,
        totals_third[0, :width],
        totals_third[1, :width],
        totals_third[2, :width],
    )


def solution(mesh):
    in_specs = (
        P(None, "dp", "row"),
        P("row", "col"),
        P("col"),
        P("col"),
        P("col"),
        P("col", "row"),
        P("row"),
        P("row"),
        P("row"),
        P(None, ("dp", "col"), "row"),
    )
    out_specs = (
        P(None, ("dp", "col"), "row"),
        P(None, ("dp", "col"), "row"),
        P("row", "col"),
        P("col"),
        P("col"),
        P("col"),
        P("col", "row"),
        P("row"),
        P("row"),
        P("row"),
    )
    return jax.shard_map(
        on_device, mesh=mesh, in_specs=in_specs, out_specs=out_specs, check_vma=False
    )
```

time: 1800 us -> 643 us (0.36)
  waiting for transfers between devices: 764 us -> 266 us
  other arithmetic: 495 us -> 47 us
  Pallas kernels: 0 us -> 224 us
  blocking collectives: 210 us -> 0 us
  local copies, waits for them, and re-layouts: 188 us -> 15.1 us
  matrix products: 98.8 us -> 0 us
  starting transfers between devices: 0.74 us -> 78 us
    reduce_scatter x4 -> x0, waiting for transfers between devices: 357 us -> none  [the longest x1 173 us: on_device(): lax.psum_scatter(partial_second, 'row', scatter_dimension=1, tiled=True)]
    while x300 -> x0, other arithmetic: 286 us -> none
    ppermute x0 -> x68, waiting for transfers between devices: none -> 266 us  [the longest x39 214 us: across(): return lax.ppermute(value, 'dp', [(i, i ^ bit) for i in range(size)])]
    psum x1 -> x0, waiting for transfers between devices: 227 us -> none  [on_device(): lax.psum((weight_grad_second, weight_grad_third), 'dp')]
    pallas_call x0 -> x19, Pallas kernels: none -> 224 us  [the longest x5 48.5 us: project(): pl.pallas_call(functools.partial(project_kernel, len(xs), len(ws), add, n...]
    psum x4 -> x0, blocking collectives: 210 us -> none  [the longest x1 75.9 us: on_device(): lax.psum((jnp.sum(norm_grad_second * unit_second, axis=(0, 1)), jnp.sum(n...]
    all_gather x3 -> x0, waiting for transfers between devices: 179 us -> none  [the longest x1 89.2 us: on_device(): hidden_full = lax.all_gather(hidden_low, 'row', axis=1, tiled=True)]
    dot_general x6 -> x0, matrix products: 98.8 us -> none  [the longest x1 25.3 us: on_device(): jnp.einsum('tsi,ij->tsj', inputs, w_second, preferred_element_type=jnp.fl...]
  transfers between devices with their start and end apart: 8 -> 68, of which waited for: 8 -> 38; matrix products, arithmetic and copies ran while one was open for 5% -> 7% of each run, Pallas kernels for 0% -> 25%
where the time goes in v1:
time: 643 us; the launch traced here: 632 us
  waiting for transfers between devices  266 us (41%)
  Pallas kernels  224 us (35%)
  starting transfers between devices  78 us (12%)
  other arithmetic  47 us (7%)
  local copies, waits for them, and re-layouts  15.1 us (2%)
    ppermute x39, waiting for transfers between devices, across(): return lax.ppermute(value, 'dp', [(i, i ^ bit) for i in range(size)])  214 us
    ppermute x39, starting transfers between devices, across(): return lax.ppermute(value, 'dp', [(i, i ^ bit) for i in range(size)])  58.5 us
    ppermute x29, waiting for transfers between devices, over(): return lax.ppermute(value, axis, [(0, 1), (1, 0)])  51.5 us
    pallas_call x5, Pallas kernels, project(): pl.pallas_call(functools.partial(project_kernel, len(xs), len(ws), add, n...  48.5 us
    pallas_call x2, Pallas kernels, pull(): pl.pallas_call(functools.partial(pull_kernel, steps, rows // seqs, count,...  46.6 us
    pallas_call x2, Pallas kernels, weight_grad(): pl.pallas_call(functools.partial(weight_kernel, steps, [b for _, _, b in...  29.8 us
    pallas_call x1, Pallas kernels, second_layer(): pl.pallas_call(functools.partial(second_layer_kernel, steps, seqs, count)...  25.4 us
    pallas_call x2, Pallas kernels, combine(): pl.pallas_call(functools.partial(combine_kernel, rows // seqs), grid_spec...  20.4 us
  transfers between devices with their start and end apart: 68, of which 38 were waited for; matrix products, arithmetic and copies ran while one was open for 7% of the time, Pallas kernels for 25%

profile of v1, /device:TPU:0, one launch (start us, length us, event | category | flops | bytes accessed | tf_op | source)
XLA Modules:
  0.0 631.9 jit_solution(11061703550282161217)
XLA Ops:
  4.7 3.0 collective-permute-start.7
  7.8 4.2 collective-permute-done.7
  12.0 3.2 collective-permute-start.8
  19.7 5.2 collective-permute-start.9
  26.3 4.7 collective-permute-done.9
  44.6 7.2 %collective-permute-done.4 = bf16[256,1024]{1,0:T(8,128)(2,1)} collective-permute-done((bf16[256,1024]{1,0:T(8,128)(2,1)}, bf16[256,1024]{1,0:T(8,128)(2,1)}, u32[]{:S(2)}, u32[]{:S(2)}) %collective-permute-start.4) | collective-permute-done | bytes 524320 | tf_op jit(solution)/shard_map/ppermute | solution.py:560
  51.8 3.0 maximum_select_fusion.1.refs_1_
  55.3 4.7 prep.2
  61.9 4.7 prep.3
  66.7 3.8 collective-permute-start.20
  70.5 10.4 %project.5 = (f32[16,912,128]{2,1,0:T(8,128)}, f32[2,2048]{1,0:T(2,128)}) custom-call(bf16[912,1024]{1,0:T(8,128)(2,1)} %get-tuple-element.53.refs_0_.a_near, bf16[1024,1024]{1,0:T(8,128)(2,1)} %copy-done, bf16[1024,1024]{1,0:T(8,128)(2,1)} %collective-permute-done.12.refs_2_.w_nf), custom_call_target="tpu_custom_call" | custom-call | tf_op jit(solution)/shard_map/project/pallas_call | solution.py:226
  84.7 10.5 %project.6 = (f32[16,912,128]{2,1,0:T(8,128)}, f32[2,2048]{1,0:T(2,128)}) custom-call(bf16[912,512]{1,0:T(8,128)(2,1)} %copy-done.8, bf16[512,1024]{1,0:T(8,128)(2,1)} %copy-done.3, bf16[512,1024]{1,0:T(8,128)(2,1)} %collective-permute-done.11.refs_2_, f32[16,912,128]{2,1,0:T(8,128)} %get-tuple-element.56.refs_3_), custom_call_target="tpu_custom_call", output_to_operand_aliasing={{0}: (3, {})} | custom-call | tf_op jit(solution)/shard_map/project/pallas_call | solution.py:226
  95.3 8.3 %collective-permute-done.refs_0_.refs_2_ = bf16[912,512]{1,0:T(8,128)(2,1)S(1)} collective-permute-done((bf16[912,512]{1,0:T(8,128)(2,1)}, bf16[912,512]{1,0:T(8,128)(2,1)S(1)}, u32[]{:S(2)}, u32[]{:S(2)}) %collective-permute-start) | collective-permute-done | bytes 933920 | tf_op jit(solution)/shard_map/ppermute | solution.py:555
  104.5 10.5 %project.7 = (f32[16,912,128]{2,1,0:T(8,128)}, f32[2,2048]{1,0:T(2,128)}) custom-call(bf16[912,512]{1,0:T(8,128)(2,1)} %copy-done.9, bf16[512,1024]{1,0:T(8,128)(2,1)} %maximum_select_fusion.1.refs_1_, bf16[512,1024]{1,0:T(8,128)(2,1)} %collective-permute-done.5.refs_2_, f32[16,912,128]{2,1,0:T(8,128)} %get-tuple-element.57.refs_3_), custom_call_target="tpu_custom_call", output_to_operand_aliasing={{0}: (3, {})} | custom-call | tf_op jit(solution)/shard_map/project/pallas_call | solution.py:226
  124.9 5.4 collective-permute-done.21
  133.0 22.9 %collective-permute-done.22 = bf16[512,1024]{1,0:T(8,128)(2,1)S(1)} collective-permute-done((bf16[512,1024]{1,0:T(8,128)(2,1)S(1)}, bf16[512,1024]{1,0:T(8,128)(2,1)S(1)}, u32[]{:S(2)}, u32[]{:S(2)}) %collective-permute-start.22) | collective-permute-done | bytes 1048608 | tf_op jit(solution)/shard_map/ppermute | solution.py:560
  159.8 5.4 prep_grads.1
  172.4 16.5 %first_layer.1 = (bf16[912,2048]{1,0:T(8,128)(2,1)}, f32[16,912,128]{2,1,0:T(8,128)}, f32[1,2048]{1,0:T(1,128)}) custom-call(f32[16,912,128]{2,1,0:T(8,128)} %get-tuple-element.58.proj, f32[2,2048]{1,0:T(2,128)} %add.226.sums, f32[3,2048]{1,0:T(4,128)} %pad_maximum_fusion.6.gains), custom_call_target="tpu_custom_call" | custom-call | tf_op jit(solution)/shard_map/first_layer/pallas_call | solution.py:342
  188.9 8.5 %project.8 = (f32[16,912,128]{2,1,0:T(8,128)}, f32[2,1024]{1,0:T(2,128)}) custom-call(bf16[912,2048]{1,0:T(8,128)(2,1)} %get-tuple-element.60.refs_0_.refs_1_.hidden, bf16[912,2048]{1,0:T(8,128)(2,1)} %get-tuple-element.60.refs_0_.refs_1_.hidden, bf16[1024,1024]{1,0:T(8,128)(2,1)} %copy-done.2, bf16[1024,1024]{1,0:T(8,128)(2,1)} %collective-permute-done.24.refs_3_.w_fn), custom_call_target="tpu_custom_call" | custom-call | tf_op jit(solution)/shard_map/project/pallas_call | solution.py:226
  198.7 8.6 %project.9 = (f32[16,912,128]{2,1,0:T(8,128)}, f32[2,1024]{1,0:T(2,128)}) custom-call(bf16[912,2048]{1,0:T(8,128)(2,1)} %get-tuple-element.60.refs_0_.refs_1_.hidden, bf16[912,2048]{1,0:T(8,128)(2,1)} %get-tuple-element.60.refs_0_.refs_1_.hidden, bf16[1024,1024]{1,0:T(8,128)(2,1)} %copy-done.1, ...), custom_call_target="tpu_custom_call", output_to_operand_aliasing={{0}: (4, {})} | custom-call | tf_op jit(solution)/shard_map/project/pallas_call | solution.py:226
  214.5 3.5 collective-permute-done.27
  229.1 25.4 %second_layer.1 = (f32[912,1024]{1,0:T(8,128)}, bf16[912,1024]{1,0:T(8,128)(2,1)}, f32[16,912,128]{2,1,0:T(8,128)}, f32[3,2048]{1,0:T(4,128)}) custom-call(f32[16,912,128]{2,1,0:T(8,128)} %get-tuple-element.63.proj, f32[2,2048]{1,0:T(2,128)} %slice.239.sums, f32[3,2048]{1,0:T(4,128)} %pad_maximum_fusion.8.gains, ...), custom_call_target="tpu_custom_call" | custom-call | tf_op jit(solution)/shard_map/second_layer/pallas_call | solution.py:374
  257.1 3.6 collective-permute-done.33
  265.0 3.7 collective-permute-done.36
  274.2 23.5 %pull.2 = (bf16[912,2048]{1,0:T(8,128)(2,1)}, f32[1,2048]{1,0:T(1,128)}, f32[16,912,128]{2,1,0:T(8,128)}) custom-call(f32[16,912,128]{2,1,0:T(8,128)} %get-tuple-element.74.arg_grads, f32[16,912,128]{2,1,0:T(8,128)} %get-tuple-element.63.proj, f32[2,2048]{1,0:T(2,128)} %slice.239.sums, f32[3,2048]{1,0:T(4,128)} %pad_maximum_fusion.8.gains, ...), custom_call_target="tpu_custom_call" | custom-call | tf_op jit(solution)/shard_map/pull/pallas_call | solution.py:458
  297.8 16.9 %first_back.1 = (f32[16,912,128]{2,1,0:T(8,128)}, f32[3,2048]{1,0:T(4,128)}) custom-call(f32[16,912,128]{2,1,0:T(8,128)} %get-tuple-element.75.grads, f32[16,912,128]{2,1,0:T(8,128)} %get-tuple-element.76.slopes, bf16[912,2048]{1,0:T(8,128)(2,1)} %get-tuple-element.60.refs_0_.refs_1_.hidden, f32[16,912,128]{2,1,0:T(8,128)} %get-tuple-element.58.proj, ...), custom_call_target="tpu_custom_call" | custom-call | tf_op jit(solution)/shard_map/first_back/pallas_call | solution.py:489
  319.7 14.7 %weight_grad.3 = (bf16[1024,1024]{1,0:T(8,128)(2,1)}, bf16[1024,1024]{1,0:T(8,128)(2,1)}, bf16[1024,1024]{1,0:T(8,128)(2,1)}, bf16[1024,1024]{1,0:T(8,128)(2,1)}) custom-call(bf16[912,2048]{1,0:T(8,128)(2,1)} %get-tuple-element.60.refs_0_.refs_1_.hidden, bf16[912,2048]{1,0:T(8,128)(2,1)} %get-tuple-element.60.refs_0_.refs_1_.hidden, ...), custom_call_target="tpu_custom_call" | custom-call | tf_op jit(solution)/shard_map/weight_grad/pallas_call | solution.py:543
  334.8 3.7 collective-permute-done.40
  344.2 3.1 pad_maximum_fusion.1.w_ff
  348.3 23.1 %pull.3 = (bf16[912,2048]{1,0:T(8,128)(2,1)}, f32[1,2048]{1,0:T(1,128)}, f32[912,1024]{1,0:T(8,128)}, bf16[912,1024]{1,0:T(8,128)(2,1)}) custom-call(f32[16,912,128]{2,1,0:T(8,128)} %get-tuple-element.77.arg_grads, f32[16,912,128]{2,1,0:T(8,128)} %get-tuple-element.58.proj, f32[2,2048]{1,0:T(2,128)} %add.226.sums, f32[3,2048]{1,0:T(4,128)} %pad_maximum_fusion.6.gains, ...), custom_call_target="tpu_custom_call" | custom-call | tf_op jit(solution)/shard_map/pull/pallas_call | solution.py:458
  371.4 15.1 %weight_grad.2 = (bf16[1024,1024]{1,0:T(8,128)(2,1)}, bf16[1024,1024]{1,0:T(8,128)(2,1)}, bf16[1024,1024]{1,0:T(8,128)(2,1)}, bf16[1024,1024]{1,0:T(8,128)(2,1)}) custom-call(bf16[912,1024]{1,0:T(8,128)(2,1)} %get-tuple-element.53.refs_0_.a_near, bf16[912,512]{1,0:T(8,128)(2,1)} %copy-done.8, bf16[912,512]{1,0:T(8,128)(2,1)} %copy-done.9, ...), custom_call_target="tpu_custom_call" | custom-call | tf_op jit(solution)/shard_map/weight_grad/pallas_call | solution.py:543
  402.8 13.0 %collective-permute-done.57 = bf16[512,1024]{1,0:T(8,128)(2,1)S(1)} collective-permute-done((bf16[512,1024]{1,0:T(8,128)(2,1)S(1)}, bf16[512,1024]{1,0:T(8,128)(2,1)S(1)}, u32[]{:S(2)}, u32[]{:S(2)}) %collective-permute-start.57) | collective-permute-done | bytes 1048608 | tf_op jit(solution)/shard_map/ppermute | solution.py:560
  416.6 21.7 %collective-permute-done.61 = bf16[512,1024]{1,0:T(8,128)(2,1)S(1)} collective-permute-done((bf16[512,1024]{1,0:T(8,128)(2,1)S(1)}, bf16[512,1024]{1,0:T(8,128)(2,1)S(1)}, u32[]{:S(2)}, u32[]{:S(2)}) %collective-permute-start.61) | collective-permute-done | bytes 1048608 | tf_op jit(solution)/shard_map/ppermute | solution.py:560
  439.2 21.6 %collective-permute-done.45 = bf16[512,1024]{1,0:T(8,128)(2,1)S(1)} collective-permute-done((bf16[512,1024]{1,0:T(8,128)(2,1)S(1)}, bf16[512,1024]{1,0:T(8,128)(2,1)S(1)}, u32[]{:S(2)}, u32[]{:S(2)}) %collective-permute-start.45) | collective-permute-done | bytes 1048608 | tf_op jit(solution)/shard_map/ppermute | solution.py:560
  461.5 21.0 %collective-permute-done.49 = bf16[512,1024]{1,0:T(8,128)(2,1)S(1)} collective-permute-done((bf16[512,1024]{1,0:T(8,128)(2,1)S(1)}, bf16[512,1024]{1,0:T(8,128)(2,1)S(1)}, u32[]{:S(2)}, u32[]{:S(2)}) %collective-permute-start.49) | collective-permute-done | bytes 1048608 | tf_op jit(solution)/shard_map/ppermute | solution.py:560
  486.9 20.7 %collective-permute-done.50 = bf16[256,1024]{1,0:T(8,128)(2,1)S(1)} collective-permute-done((bf16[256,1024]{1,0:T(8,128)(2,1)S(1)}, bf16[256,1024]{1,0:T(8,128)(2,1)S(1)}, u32[]{:S(2)}, u32[]{:S(2)}) %collective-permute-start.50) | collective-permute-done | bytes 524320 | tf_op jit(solution)/shard_map/ppermute | solution.py:560
  510.1 3.0 collective-permute-start.47
  513.0 10.2 %collective-permute-done.51 = bf16[128,1024]{1,0:T(8,128)(2,1)S(1)} collective-permute-done((bf16[128,1024]{1,0:T(8,128)(2,1)S(1)}, bf16[128,1024]{1,0:T(8,128)(2,1)S(1)}, u32[]{:S(2)}, u32[]{:S(2)}) %collective-permute-start.51) | collective-permute-done | bytes 262176 | tf_op jit(solution)/shard_map/ppermute | solution.py:560
  527.6 7.0 %collective-permute-done.47 = bf16[128,1024]{1,0:T(8,128)(2,1)S(1)} collective-permute-done((bf16[128,1024]{1,0:T(8,128)(2,1)S(1)}, bf16[128,1024]{1,0:T(8,128)(2,1)S(1)}, u32[]{:S(2)}, u32[]{:S(2)}) %collective-permute-start.47) | collective-permute-done | bytes 262176 | tf_op jit(solution)/shard_map/ppermute | solution.py:560
  534.7 11.0 %collective-permute-done.65 = bf16[128,1024]{1,0:T(8,128)(2,1)S(1)} collective-permute-done((bf16[128,1024]{1,0:T(8,128)(2,1)S(1)}, bf16[128,1024]{1,0:T(8,128)(2,1)S(1)}, u32[]{:S(2)}, u32[]{:S(2)}) %collective-permute-start.65) | collective-permute-done | bytes 262176 | tf_op jit(solution)/shard_map/ppermute | solution.py:560
  545.9 4.8 collective-permute-start.66
  550.7 3.5 collective-permute-done.53
  554.6 10.1 %collective-permute-done.66 = bf16[256,1024]{1,0:T(8,128)(2,1)S(1)} collective-permute-done((bf16[256,1024]{1,0:T(8,128)(2,1)S(1)}, bf16[256,1024]{1,0:T(8,128)(2,1)S(1)}, u32[]{:S(2)}, u32[]{:S(2)}) %collective-permute-start.66) | collective-permute-done | bytes 524320 | tf_op jit(solution)/shard_map/ppermute | solution.py:560
  565.7 8.0 %collective-permute-done.54 = bf16[256,1024]{1,0:T(8,128)(2,1)S(1)} collective-permute-done((bf16[256,1024]{1,0:T(8,128)(2,1)S(1)}, bf16[256,1024]{1,0:T(8,128)(2,1)S(1)}, u32[]{:S(2)}, u32[]{:S(2)}) %collective-permute-start.54) | collective-permute-done | bytes 524320 | tf_op jit(solution)/shard_map/ppermute | solution.py:560
  578.2 10.1 %combine.2 = f32[12,150,1000]{2,1,0:T(8,128)} custom-call(s32[2]{0:T(128)} %pad_add_fusion.at_ref, bf16[912,1024]{1,0:T(8,128)(2,1)} %get-tuple-element.53.refs_0_.a_near, f32[912,1024]{1,0:T(8,128)} %get-tuple-element.70.b_near, bf16[912,512]{1,0:T(8,128)(2,1)} %get-tuple-element.55.a_far0, bf16[912,512]{1,0:T(8,128)(2,1)} %get-tuple-element.54.a_far1, ...), custom_call_target="tpu_custom_call" | custom-call | tf_op jit(solution)/shard_map/combine/pallas_call | solution.py:146
  588.3 23.4 %collective-permute-done.43.b_far = bf16[912,1024]{1,0:T(8,128)(2,1)S(1)} collective-permute-done((bf16[912,1024]{1,0:T(8,128)(2,1)}, bf16[912,1024]{1,0:T(8,128)(2,1)S(1)}, u32[]{:S(2)}, u32[]{:S(2)}) %collective-permute-start.43) | collective-permute-done | bytes 1867808 | tf_op jit(solution)/shard_map/ppermute | solution.py:555
  612.9 10.3 %combine.3 = f32[12,150,1000]{2,1,0:T(8,128)} custom-call(s32[2]{0:T(128)} %pad_add_fusion.at_ref, bf16[912,1024]{1,0:T(8,128)(2,1)} %get-tuple-element.68.cot_near.a_near, f32[912,1024]{1,0:T(8,128)} %get-tuple-element.80.b_near, bf16[912,1024]{1,0:T(8,128)(2,1)} %get-tuple-element.69.a_far0.a_far1, bf16[912,1024]{1,0:T(8,128)(2,1)} %get-tuple-element.69.a_far0.a_far1, ...), custom_call_target="tpu_custom_call" | custom-call | tf_op jit(solution)/shard_map/combine/pallas_call | solution.py:146
  623.2 5.3 multiply_add_fusion
  (259 shorter events, 138.2 us)
Async XLA Ops:
  7.7 7.8 %collective-permute-start.1 = (bf16[64,1024]{1,0:T(8,128)(2,1)S(1)}, bf16[64,1024]{1,0:T(8,128)(2,1)S(1)}, u32[]{:S(2)}, u32[]{:S(2)}) collective-permute-start(bf16[64,1024]{1,0:T(8,128)(2,1)S(1)} %get-tuple-element.95), channel_id=1, source_target_pairs={{0,2},{2,0},{1,3},{3,1},{4,6},{6,4},{5,7},{7,5},{8,10},{10,8},{9,1... | collective-permute-start | bytes 393224 | tf_op jit(solution)/shard_map/ppermute | solution.py:555
  15.4 51.3 %collective-permute-start.12 = (bf16[1024,1024]{1,0:T(8,128)(2,1)S(1)}, bf16[1024,1024]{1,0:T(8,128)(2,1)}, u32[]{:S(2)}, u32[]{:S(2)}) collective-permute-start(bf16[1024,1024]{1,0:T(8,128)(2,1)S(1)} %pad.15.refs_1_.w_nn), channel_id=1, source_target_pairs={{0,1},{1,0},{2,3},{3,2},{4,5},{5,4},{6,7},{7,6},{8,9},{9,8},{10,11... | collective-permute-start | bytes 6291464 | tf_op jit(solution)/shard_map/ppermute | solution.py:555
  15.5 9.7 %collective-permute-start.2 = (bf16[64,1024]{1,0:T(8,128)(2,1)S(1)}, bf16[64,1024]{1,0:T(8,128)(2,1)S(1)}, u32[]{:S(2)}, u32[]{:S(2)}) collective-permute-start(bf16[64,1024]{1,0:T(8,128)(2,1)S(1)} %collective-permute-done.1), channel_id=1, source_target_pairs={{0,16},{4,20},{8,24},{12,28},{16,0},{20,4},{24,8},{28,12},{1,17},{... | collective-permute-start | bytes 393224 | tf_op jit(solution)/shard_map/ppermute | solution.py:560
  19.7 11.3 %collective-permute-start.9 = (bf16[128,1024]{1,0:T(8,128)(2,1)S(1)}, bf16[128,1024]{1,0:T(8,128)(2,1)S(1)}, u32[]{:S(2)}, u32[]{:S(2)}) collective-permute-start(bf16[128,1024]{1,0:T(8,128)(2,1)S(1)} %maximum_select_fusion.12), channel_id=1, source_target_pairs={{0,8},{4,12},{8,0},{12,4},{16,24},{20,28},{24,16},{28,20},{1,9},{5... | collective-permute-start | bytes 786440 | tf_op jit(solution)/shard_map/ppermute | solution.py:560
  25.3 9.7 %collective-permute-start.3 = (bf16[128,1024]{1,0:T(8,128)(2,1)S(1)}, bf16[128,1024]{1,0:T(8,128)(2,1)}, u32[]{:S(2)}, u32[]{:S(2)}) collective-permute-start(bf16[128,1024]{1,0:T(8,128)(2,1)S(1)} %maximum_select_fusion.11), channel_id=1, source_target_pairs={{0,8},{4,12},{8,0},{12,4},{16,24},{20,28},{24,16},{28,20},{1,9},{5... | collective-permute-start | bytes 786440 | tf_op jit(solution)/shard_map/ppermute | solution.py:560
  31.2 11.2 %collective-permute-start.10 = (bf16[256,1024]{1,0:T(8,128)(2,1)S(1)}, bf16[256,1024]{1,0:T(8,128)(2,1)}, u32[]{:S(2)}, u32[]{:S(2)}) collective-permute-start(bf16[256,1024]{1,0:T(8,128)(2,1)S(1)} %maximum_select_fusion.7), channel_id=1, source_target_pairs={{0,4},{4,0},{8,12},{12,8},{16,20},{20,16},{24,28},{28,24},{1,5},{5... | collective-permute-start | bytes 1572872 | tf_op jit(solution)/shard_map/ppermute | solution.py:560
  37.0 14.8 %collective-permute-start.4 = (bf16[256,1024]{1,0:T(8,128)(2,1)}, bf16[256,1024]{1,0:T(8,128)(2,1)}, u32[]{:S(2)}, u32[]{:S(2)}) collective-permute-start(bf16[256,1024]{1,0:T(8,128)(2,1)} %maximum_select_fusion.6), channel_id=1, source_target_pairs={{0,4},{4,0},{8,12},{12,8},{16,20},{20,16},{24,28},{28,24},{1,5},{5... | collective-permute-start | bytes 1572872 | tf_op jit(solution)/shard_map/ppermute | solution.py:560
  40.9 25.7 %collective-permute-start.19 = (bf16[128,1024]{1,0:T(8,128)(2,1)}, bf16[128,1024]{1,0:T(8,128)(2,1)S(1)}, u32[]{:S(2)}, u32[]{:S(2)}) collective-permute-start(bf16[128,1024]{1,0:T(8,128)(2,1)} %cut.3), channel_id=1, source_target_pairs={{0,2},{2,0},{1,3},{3,1},{4,6},{6,4},{5,7},{7,5},{8,10},{10,8},{9,1... | collective-permute-start | bytes 786440 | tf_op jit(solution)/shard_map/ppermute | solution.py:555
  44.5 39.3 %collective-permute-start.11 = (bf16[512,1024]{1,0:T(8,128)(2,1)S(1)}, bf16[512,1024]{1,0:T(8,128)(2,1)}, u32[]{:S(2)}, u32[]{:S(2)}) collective-permute-start(bf16[512,1024]{1,0:T(8,128)(2,1)S(1)} %maximum_select_fusion.2.refs_1_), channel_id=1, source_target_pairs={{0,1},{1,0},{2,3},{3,2},{4,5},{5,4},{6,7},{7,6},{8,9},{9,8},{10,11... | collective-permute-start | bytes 3145736 | tf_op jit(solution)/shard_map/ppermute | solution.py:555
  54.7 48.8 %collective-permute-start.5 = (bf16[512,1024]{1,0:T(8,128)(2,1)}, bf16[512,1024]{1,0:T(8,128)(2,1)}, u32[]{:S(2)}, u32[]{:S(2)}) collective-permute-start(bf16[512,1024]{1,0:T(8,128)(2,1)} %maximum_select_fusion.1.refs_1_), channel_id=1, source_target_pairs={{0,1},{1,0},{2,3},{3,2},{4,5},{5,4},{6,7},{7,6},{8,9},{9,8},{10,11... | collective-permute-start | bytes 3145736 | tf_op jit(solution)/shard_map/ppermute | solution.py:555
  60.0 23.8 %collective-permute-start.6 = (bf16[912,512]{1,0:T(8,128)(2,1)}, bf16[912,512]{1,0:T(8,128)(2,1)S(1)}, u32[]{:S(2)}, u32[]{:S(2)}) collective-permute-start(bf16[912,512]{1,0:T(8,128)(2,1)} %get-tuple-element.55.a_far0), channel_id=1, source_target_pairs={{0,2},{2,0},{1,3},{3,1},{4,6},{6,4},{5,7},{7,5},{8,10},{10,8},{9,1... | collective-permute-start | bytes 2801672 | tf_op jit(solution)/shard_map/ppermute | solution.py:555
  66.6 36.9 %collective-permute-start = (bf16[912,512]{1,0:T(8,128)(2,1)}, bf16[912,512]{1,0:T(8,128)(2,1)S(1)}, u32[]{:S(2)}, u32[]{:S(2)}) collective-permute-start(bf16[912,512]{1,0:T(8,128)(2,1)} %get-tuple-element.54.a_far1), channel_id=1, source_target_pairs={{0,2},{2,0},{1,3},{3,1},{4,6},{6,4},{5,7},{7,5},{8,10},{10,8},{9,1... | collective-permute-start | bytes 2801672 | tf_op jit(solution)/shard_map/ppermute | solution.py:555
  66.7 48.3 %collective-permute-start.20 = (bf16[128,1024]{1,0:T(8,128)(2,1)S(1)}, bf16[128,1024]{1,0:T(8,128)(2,1)S(1)}, u32[]{:S(2)}, u32[]{:S(2)}) collective-permute-start(bf16[128,1024]{1,0:T(8,128)(2,1)S(1)} %collective-permute-done.19), channel_id=1, source_target_pairs={{0,16},{4,20},{8,24},{12,28},{16,0},{20,4},{24,8},{28,12},{1,17},{... | collective-permute-start | bytes 786440 | tf_op jit(solution)/shard_map/ppermute | solution.py:560
  115.2 15.1 %collective-permute-start.21 = (bf16[256,1024]{1,0:T(8,128)(2,1)S(1)}, bf16[256,1024]{1,0:T(8,128)(2,1)S(1)}, u32[]{:S(2)}, u32[]{:S(2)}) collective-permute-start(bf16[256,1024]{1,0:T(8,128)(2,1)S(1)} %maximum_select_fusion.8), channel_id=1, source_target_pairs={{0,8},{4,12},{8,0},{12,4},{16,24},{20,28},{24,16},{28,20},{1,9},{5... | collective-permute-start | bytes 1572872 | tf_op jit(solution)/shard_map/ppermute | solution.py:560
  123.0 7.8 %collective-permute-start.15 = (f32[2,2048]{1,0:T(2,128)S(1)}, f32[2,2048]{1,0:T(2,128)S(1)}, u32[]{:S(2)}, u32[]{:S(2)}) collective-permute-start(f32[2,2048]{1,0:T(2,128)S(1)} %fusion.16), channel_id=1, source_target_pairs={{0,4},{4,0},{8,12},{12,8},{16,20},{20,16},{24,28},{28,24},{1,5},{5... | collective-permute-start | bytes 49160 | tf_op jit(solution)/shard_map/ppermute | solution.py:560
  130.8 25.1 %collective-permute-start.22 = (bf16[512,1024]{1,0:T(8,128)(2,1)S(1)}, bf16[512,1024]{1,0:T(8,128)(2,1)S(1)}, u32[]{:S(2)}, u32[]{:S(2)}) collective-permute-start(bf16[512,1024]{1,0:T(8,128)(2,1)S(1)} %maximum_select_fusion.3), channel_id=1, source_target_pairs={{0,4},{4,0},{8,12},{12,8},{16,20},{20,16},{24,28},{28,24},{1,5},{5... | collective-permute-start | bytes 3145736 | tf_op jit(solution)/shard_map/ppermute | solution.py:560
  133.0 55.9 %collective-permute-start.24 = (bf16[1024,1024]{1,0:T(8,128)(2,1)S(1)}, bf16[1024,1024]{1,0:T(8,128)(2,1)}, u32[]{:S(2)}, u32[]{:S(2)}) collective-permute-start(bf16[1024,1024]{1,0:T(8,128)(2,1)S(1)} %pad.17.refs_2_.w_nn), channel_id=1, source_target_pairs={{0,1},{1,0},{2,3},{3,2},{4,5},{5,4},{6,7},{7,6},{8,9},{9,8},{10,11... | collective-permute-start | bytes 6291464 | tf_op jit(solution)/shard_map/ppermute | solution.py:555
  156.9 40.4 %collective-permute-start.23 = (bf16[1024,1024]{1,0:T(8,128)(2,1)S(1)}, bf16[1024,1024]{1,0:T(8,128)(2,1)S(1)}, u32[]{:S(2)}, u32[]{:S(2)}) collective-permute-start(bf16[1024,1024]{1,0:T(8,128)(2,1)S(1)} %maximum_select_fusion.refs_2_.w_nf), channel_id=1, source_target_pairs={{0,1},{1,0},{2,3},{3,2},{4,5},{5,4},{6,7},{7,6},{8,9},{9,8},{10,11... | collective-permute-start | bytes 6291464 | tf_op jit(solution)/shard_map/ppermute | solution.py:555
  157.1 12.6 %collective-permute-start.18 = (f32[3,1024]{1,0:T(4,128)S(1)}, f32[3,1024]{1,0:T(4,128)S(1)}, u32[]{:S(2)}, u32[]{:S(2)}) collective-permute-start(f32[3,1024]{1,0:T(4,128)S(1)} %select_maximum_fusion.2), channel_id=1, source_target_pairs={{0,1},{1,0},{2,3},{3,2},{4,5},{5,4},{6,7},{7,6},{8,9},{9,8},{10,11... | collective-permute-start | bytes 36872 | tf_op jit(solution)/shard_map/ppermute | solution.py:555
  157.6 9.3 %collective-permute-start.16 = (f32[2,2048]{1,0:T(2,128)S(1)}, f32[2,2048]{1,0:T(2,128)S(1)}, u32[]{:S(2)}, u32[]{:S(2)}) collective-permute-start(f32[2,2048]{1,0:T(2,128)S(1)} %add.224), channel_id=1, source_target_pairs={{0,8},{4,12},{8,0},{12,4},{16,24},{20,28},{24,16},{28,20},{1,9},{5... | collective-permute-start | bytes 49160 | tf_op jit(solution)/shard_map/ppermute | solution.py:560
  165.2 62.6 %collective-permute-start.31 = (bf16[912,1024]{1,0:T(8,128)(2,1)}, bf16[912,1024]{1,0:T(8,128)(2,1)S(1)}, u32[]{:S(2)}, u32[]{:S(2)}) collective-permute-start(bf16[912,1024]{1,0:T(8,128)(2,1)} %get-tuple-element.69.a_far0.a_far1), channel_id=1, source_target_pairs={{0,2},{2,0},{1,3},{3,1},{4,6},{6,4},{5,7},{7,5},{8,10},{10,8},{9,1... | collective-permute-start | bytes 5603336 | tf_op jit(solution)/shard_map/ppermute | solution.py:555
  317.5 16.9 %collective-permute-start.39 = (f32[4,2048]{1,0:T(4,128)S(1)}, f32[4,2048]{1,0:T(4,128)S(1)}, u32[]{:S(2)}, u32[]{:S(2)}) collective-permute-start(f32[4,2048]{1,0:T(4,128)S(1)} %maximum_add_fusion.3), channel_id=1, source_target_pairs={{0,4},{4,0},{8,12},{12,8},{16,20},{20,16},{24,28},{28,24},{1,5},{5... | collective-permute-start | bytes 98312 | tf_op jit(solution)/shard_map/ppermute | solution.py:560
  334.4 52.7 %collective-permute-start.56 = (bf16[1024,1024]{1,0:T(8,128)(2,1)}, bf16[1024,1024]{1,0:T(8,128)(2,1)}, u32[]{:S(2)}, u32[]{:S(2)}) collective-permute-start(bf16[1024,1024]{1,0:T(8,128)(2,1)} %get-tuple-element.89), channel_id=1, source_target_pairs={{0,1},{1,0},{2,3},{3,2},{4,5},{5,4},{6,7},{7,6},{8,9},{9,8},{10,11... | collective-permute-start | bytes 6291464 | tf_op jit(solution)/shard_map/ppermute | solution.py:555
  347.3 43.0 %collective-permute-start.60 = (bf16[1024,1024]{1,0:T(8,128)(2,1)}, bf16[1024,1024]{1,0:T(8,128)(2,1)}, u32[]{:S(2)}, u32[]{:S(2)}) collective-permute-start(bf16[1024,1024]{1,0:T(8,128)(2,1)} %get-tuple-element.92), channel_id=1, source_target_pairs={{0,1},{1,0},{2,3},{3,2},{4,5},{5,4},{6,7},{7,6},{8,9},{9,8},{10,11... | collective-permute-start | bytes 6291464 | tf_op jit(solution)/shard_map/ppermute | solution.py:555
  386.5 8.1 %collective-permute-start.44 = (bf16[1024,1024]{1,0:T(8,128)(2,1)}, bf16[1024,1024]{1,0:T(8,128)(2,1)}, u32[]{:S(2)}, u32[]{:S(2)}) collective-permute-start(bf16[1024,1024]{1,0:T(8,128)(2,1)} %get-tuple-element.84), channel_id=1, source_target_pairs={{0,1},{1,0},{2,3},{3,2},{4,5},{5,4},{6,7},{7,6},{8,9},{9,8},{10,11... | collective-permute-start | bytes 6291464 | tf_op jit(solution)/shard_map/ppermute | solution.py:555
  386.8 11.9 %collective-permute-start.48 = (bf16[1024,1024]{1,0:T(8,128)(2,1)}, bf16[1024,1024]{1,0:T(8,128)(2,1)}, u32[]{:S(2)}, u32[]{:S(2)}) collective-permute-start(bf16[1024,1024]{1,0:T(8,128)(2,1)} %get-tuple-element.86), channel_id=1, source_target_pairs={{0,1},{1,0},{2,3},{3,2},{4,5},{5,4},{6,7},{7,6},{8,9},{9,8},{10,11... | collective-permute-start | bytes 6291464 | tf_op jit(solution)/shard_map/ppermute | solution.py:555
  389.8 26.1 %collective-permute-start.57 = (bf16[512,1024]{1,0:T(8,128)(2,1)S(1)}, bf16[512,1024]{1,0:T(8,128)(2,1)S(1)}, u32[]{:S(2)}, u32[]{:S(2)}) collective-permute-start(bf16[512,1024]{1,0:T(8,128)(2,1)S(1)} %dynamic-slice_convert_fusion.1), channel_id=1, source_target_pairs={{0,4},{4,0},{8,12},{12,8},{16,20},{20,16},{24,28},{28,24},{1,5},{5... | collective-permute-start | bytes 3145736 | tf_op jit(solution)/shard_map/ppermute | solution.py:560
  393.9 44.4 %collective-permute-start.61 = (bf16[512,1024]{1,0:T(8,128)(2,1)S(1)}, bf16[512,1024]{1,0:T(8,128)(2,1)S(1)}, u32[]{:S(2)}, u32[]{:S(2)}) collective-permute-start(bf16[512,1024]{1,0:T(8,128)(2,1)S(1)} %dynamic-slice_convert_fusion), channel_id=1, source_target_pairs={{0,4},{4,0},{8,12},{12,8},{16,20},{20,16},{24,28},{28,24},{1,5},{5... | collective-permute-start | bytes 3145736 | tf_op jit(solution)/shard_map/ppermute | solution.py:560
  398.0 62.8 %collective-permute-start.45 = (bf16[512,1024]{1,0:T(8,128)(2,1)S(1)}, bf16[512,1024]{1,0:T(8,128)(2,1)S(1)}, u32[]{:S(2)}, u32[]{:S(2)}) collective-permute-start(bf16[512,1024]{1,0:T(8,128)(2,1)S(1)} %dynamic-slice_convert_fusion.3), channel_id=1, source_target_pairs={{0,4},{4,0},{8,12},{12,8},{16,20},{20,16},{24,28},{28,24},{1,5},{5... | collective-permute-start | bytes 3145736 | tf_op jit(solution)/shard_map/ppermute | solution.py:560
  402.1 80.5 %collective-permute-start.49 = (bf16[512,1024]{1,0:T(8,128)(2,1)S(1)}, bf16[512,1024]{1,0:T(8,128)(2,1)S(1)}, u32[]{:S(2)}, u32[]{:S(2)}) collective-permute-start(bf16[512,1024]{1,0:T(8,128)(2,1)S(1)} %dynamic-slice_convert_fusion.2), channel_id=1, source_target_pairs={{0,4},{4,0},{8,12},{12,8},{16,20},{20,16},{24,28},{28,24},{1,5},{5... | collective-permute-start | bytes 3145736 | tf_op jit(solution)/shard_map/ppermute | solution.py:560
  416.2 67.2 %collective-permute-start.58 = (bf16[256,1024]{1,0:T(8,128)(2,1)S(1)}, bf16[256,1024]{1,0:T(8,128)(2,1)S(1)}, u32[]{:S(2)}, u32[]{:S(2)}) collective-permute-start(bf16[256,1024]{1,0:T(8,128)(2,1)S(1)} %dynamic-slice_convert_fusion.5), channel_id=1, source_target_pairs={{0,8},{4,12},{8,0},{12,4},{16,24},{20,28},{24,16},{28,20},{1,9},{5... | collective-permute-start | bytes 1572872 | tf_op jit(solution)/shard_map/ppermute | solution.py:560
  438.9 46.9 %collective-permute-start.62 = (bf16[256,1024]{1,0:T(8,128)(2,1)S(1)}, bf16[256,1024]{1,0:T(8,128)(2,1)S(1)}, u32[]{:S(2)}, u32[]{:S(2)}) collective-permute-start(bf16[256,1024]{1,0:T(8,128)(2,1)S(1)} %dynamic-slice_convert_fusion.4), channel_id=1, source_target_pairs={{0,8},{4,12},{8,0},{12,4},{16,24},{20,28},{24,16},{28,20},{1,9},{5... | collective-permute-start | bytes 1572872 | tf_op jit(solution)/shard_map/ppermute | solution.py:560
  461.2 46.7 %collective-permute-start.46 = (bf16[256,1024]{1,0:T(8,128)(2,1)S(1)}, bf16[256,1024]{1,0:T(8,128)(2,1)S(1)}, u32[]{:S(2)}, u32[]{:S(2)}) collective-permute-start(bf16[256,1024]{1,0:T(8,128)(2,1)S(1)} %dynamic-slice_convert_fusion.7), channel_id=1, source_target_pairs={{0,8},{4,12},{8,0},{12,4},{16,24},{20,28},{24,16},{28,20},{1,9},{5... | collective-permute-start | bytes 1572872 | tf_op jit(solution)/shard_map/ppermute | solution.py:560
  483.1 24.5 %collective-permute-start.50 = (bf16[256,1024]{1,0:T(8,128)(2,1)S(1)}, bf16[256,1024]{1,0:T(8,128)(2,1)S(1)}, u32[]{:S(2)}, u32[]{:S(2)}) collective-permute-start(bf16[256,1024]{1,0:T(8,128)(2,1)S(1)} %dynamic-slice_convert_fusion.6), channel_id=1, source_target_pairs={{0,8},{4,12},{8,0},{12,4},{16,24},{20,28},{24,16},{28,20},{1,9},{5... | collective-permute-start | bytes 1572872 | tf_op jit(solution)/shard_map/ppermute | solution.py:560
  483.6 41.6 %collective-permute-start.59 = (bf16[128,1024]{1,0:T(8,128)(2,1)S(1)}, bf16[128,1024]{1,0:T(8,128)(2,1)S(1)}, u32[]{:S(2)}, u32[]{:S(2)}) collective-permute-start(bf16[128,1024]{1,0:T(8,128)(2,1)S(1)} %dynamic-slice_convert_fusion.9), channel_id=1, source_target_pairs={{0,16},{4,20},{8,24},{12,28},{16,0},{20,4},{24,8},{28,12},{1,17},{... | collective-permute-start | bytes 786440 | tf_op jit(solution)/shard_map/ppermute | solution.py:560
  486.0 22.1 %collective-permute-start.63 = (bf16[128,1024]{1,0:T(8,128)(2,1)S(1)}, bf16[128,1024]{1,0:T(8,128)(2,1)S(1)}, u32[]{:S(2)}, u32[]{:S(2)}) collective-permute-start(bf16[128,1024]{1,0:T(8,128)(2,1)S(1)} %dynamic-slice_convert_fusion.8), channel_id=1, source_target_pairs={{0,16},{4,20},{8,24},{12,28},{16,0},{20,4},{24,8},{28,12},{1,17},{... | collective-permute-start | bytes 786440 | tf_op jit(solution)/shard_map/ppermute | solution.py:560
  507.8 15.4 %collective-permute-start.51 = (bf16[128,1024]{1,0:T(8,128)(2,1)S(1)}, bf16[128,1024]{1,0:T(8,128)(2,1)S(1)}, u32[]{:S(2)}, u32[]{:S(2)}) collective-permute-start(bf16[128,1024]{1,0:T(8,128)(2,1)S(1)} %dynamic-slice_convert_fusion.10), channel_id=1, source_target_pairs={{0,16},{4,20},{8,24},{12,28},{16,0},{20,4},{24,8},{28,12},{1,17},{... | collective-permute-start | bytes 786440 | tf_op jit(solution)/shard_map/ppermute | solution.py:560
  508.2 17.1 %collective-permute-start.64 = (bf16[128,1024]{1,0:T(8,128)(2,1)S(1)}, bf16[128,1024]{1,0:T(8,128)(2,1)S(1)}, u32[]{:S(2)}, u32[]{:S(2)}) collective-permute-start(bf16[128,1024]{1,0:T(8,128)(2,1)S(1)} %add_convert_fusion.1), channel_id=1, source_target_pairs={{0,2},{2,0},{1,3},{3,1},{4,6},{6,4},{5,7},{7,5},{8,10},{10,8},{9,1... | collective-permute-start | bytes 786440 | tf_op jit(solution)/shard_map/ppermute | solution.py:555
  510.1 24.4 %collective-permute-start.47 = (bf16[128,1024]{1,0:T(8,128)(2,1)S(1)}, bf16[128,1024]{1,0:T(8,128)(2,1)S(1)}, u32[]{:S(2)}, u32[]{:S(2)}) collective-permute-start(bf16[128,1024]{1,0:T(8,128)(2,1)S(1)} %dynamic-slice_convert_fusion.11), channel_id=1, source_target_pairs={{0,16},{4,20},{8,24},{12,28},{16,0},{20,4},{24,8},{28,12},{1,17},{... | collective-permute-start | bytes 786440 | tf_op jit(solution)/shard_map/ppermute | solution.py:560
  523.4 11.2 %collective-permute-start.52 = (bf16[128,1024]{1,0:T(8,128)(2,1)S(1)}, bf16[128,1024]{1,0:T(8,128)(2,1)S(1)}, u32[]{:S(2)}, u32[]{:S(2)}) collective-permute-start(bf16[128,1024]{1,0:T(8,128)(2,1)S(1)} %add_convert_fusion.3), channel_id=1, source_target_pairs={{0,2},{2,0},{1,3},{3,1},{4,6},{6,4},{5,7},{7,5},{8,10},{10,8},{9,1... | collective-permute-start | bytes 786440 | tf_op jit(solution)/shard_map/ppermute | solution.py:555
  525.4 20.4 %collective-permute-start.65 = (bf16[128,1024]{1,0:T(8,128)(2,1)S(1)}, bf16[128,1024]{1,0:T(8,128)(2,1)S(1)}, u32[]{:S(2)}, u32[]{:S(2)}) collective-permute-start(bf16[128,1024]{1,0:T(8,128)(2,1)S(1)} %add_convert_fusion), channel_id=1, source_target_pairs={{0,16},{4,20},{8,24},{12,28},{16,0},{20,4},{24,8},{28,12},{1,17},{... | collective-permute-start | bytes 786440 | tf_op jit(solution)/shard_map/ppermute | solution.py:560
  525.5 51.4 %collective-permute-start.34 = (bf16[912,1024]{1,0:T(8,128)(2,1)S(1)}, bf16[912,1024]{1,0:T(8,128)(2,1)S(1)}, u32[]{:S(2)}, u32[]{:S(2)}) collective-permute-start(bf16[912,1024]{1,0:T(8,128)(2,1)S(1)} %copy-done.29), channel_id=1, source_target_pairs={{0,2},{2,0},{1,3},{3,1},{4,6},{6,4},{5,7},{7,5},{8,10},{10,8},{9,1... | collective-permute-start | bytes 5603336 | tf_op jit(solution)/shard_map/ppermute | solution.py:555
  525.7 86.0 %collective-permute-start.43 = (bf16[912,1024]{1,0:T(8,128)(2,1)}, bf16[912,1024]{1,0:T(8,128)(2,1)S(1)}, u32[]{:S(2)}, u32[]{:S(2)}) collective-permute-start(bf16[912,1024]{1,0:T(8,128)(2,1)} %get-tuple-element.81), channel_id=1, source_target_pairs={{0,2},{2,0},{1,3},{3,1},{4,6},{6,4},{5,7},{7,5},{8,10},{10,8},{9,1... | collective-permute-start | bytes 5603336 | tf_op jit(solution)/shard_map/ppermute | solution.py:555
  534.6 19.6 %collective-permute-start.53 = (bf16[128,1024]{1,0:T(8,128)(2,1)S(1)}, bf16[128,1024]{1,0:T(8,128)(2,1)S(1)}, u32[]{:S(2)}, u32[]{:S(2)}) collective-permute-start(bf16[128,1024]{1,0:T(8,128)(2,1)S(1)} %add_convert_fusion.2), channel_id=1, source_target_pairs={{0,16},{4,20},{8,24},{12,28},{16,0},{20,4},{24,8},{28,12},{1,17},{... | collective-permute-start | bytes 786440 | tf_op jit(solution)/shard_map/ppermute | solution.py:560
  545.9 18.7 %collective-permute-start.66 = (bf16[256,1024]{1,0:T(8,128)(2,1)S(1)}, bf16[256,1024]{1,0:T(8,128)(2,1)S(1)}, u32[]{:S(2)}, u32[]{:S(2)}) collective-permute-start(bf16[256,1024]{1,0:T(8,128)(2,1)S(1)} %maximum_select_fusion.10), channel_id=1, source_target_pairs={{0,8},{4,12},{8,0},{12,4},{16,24},{20,28},{24,16},{28,20},{1,9},{5... | collective-permute-start | bytes 1572872 | tf_op jit(solution)/shard_map/ppermute | solution.py:560
  554.3 19.4 %collective-permute-start.54 = (bf16[256,1024]{1,0:T(8,128)(2,1)S(1)}, bf16[256,1024]{1,0:T(8,128)(2,1)S(1)}, u32[]{:S(2)}, u32[]{:S(2)}) collective-permute-start(bf16[256,1024]{1,0:T(8,128)(2,1)S(1)} %maximum_select_fusion.9), channel_id=1, source_target_pairs={{0,8},{4,12},{8,0},{12,4},{16,24},{20,28},{24,16},{28,20},{1,9},{5... | collective-permute-start | bytes 1572872 | tf_op jit(solution)/shard_map/ppermute | solution.py:560
  565.1 58.1 %collective-permute-start.67 = (bf16[512,1024]{1,0:T(8,128)(2,1)S(1)}, bf16[512,1024]{1,0:T(8,128)(2,1)S(1)}, u32[]{:S(2)}, u32[]{:S(2)}) collective-permute-start(bf16[512,1024]{1,0:T(8,128)(2,1)S(1)} %maximum_select_fusion.5), channel_id=1, source_target_pairs={{0,4},{4,0},{8,12},{12,8},{16,20},{20,16},{24,28},{28,24},{1,5},{5... | collective-permute-start | bytes 3145736 | tf_op jit(solution)/shard_map/ppermute | solution.py:560
  574.2 54.3 %collective-permute-start.55 = (bf16[512,1024]{1,0:T(8,128)(2,1)S(1)}, bf16[512,1024]{1,0:T(8,128)(2,1)S(1)}, u32[]{:S(2)}, u32[]{:S(2)}) collective-permute-start(bf16[512,1024]{1,0:T(8,128)(2,1)S(1)} %maximum_select_fusion.4), channel_id=1, source_target_pairs={{0,4},{4,0},{8,12},{12,8},{16,20},{20,16},{24,28},{28,24},{1,5},{5... | collective-permute-start | bytes 3145736 | tf_op jit(solution)/shard_map/ppermute | solution.py:560
  (51 other events, 482.8 us)
